TPU v7x, 256 devices: a whole 4x4x8 slice. The times are simulated.
256 devices in a mesh: tm: 16 (over z_hi, y), sx: 4 (over z_lo, core), sy: 4 (over x).
Axes of the slice: x: 4, y: 4, z: 8 (z_hi: 4, z_lo: 2; z = z_hi * 2 + z_lo), core: 2. Of those that a mesh axis runs over, the one named last changes fastest.
Arguments:
- start: float32 [32, 128, 256], P('sx', 'sy'), may hold values from -6 to 6
- guess: float32 [16, 32, 128, 256], P('tm', 'sx', 'sy'), may hold values from -10 to 10
- forcing: float32 [64, 32, 128, 256], P('tm', 'sx', 'sy'), may hold values from -8 to 8
- absorb: float32 [32, 128, 256], P('sx', 'sy'), may hold values from 0.004 to 0.25
Outputs:
- solution: float32 [64, 32, 128, 256], P('tm', 'sx', 'sy')
All inputs are finite; a program needn't handle non-finite values.
Results may differ from a plain program's by a relative error of at most 0.00006.
Values sent between devices are 32-bit elements; how exact they have to be, the bound alone decides.
No kernel may reach another device: no remote copies, remote signals or barrier semaphores. Data moves between devices by JAX's collectives and lax.ppermute only.
A program may use at most 64 MiB of HBM per device.

v0:
```python
import jax
import jax.numpy as jnp
from jax import lax
from jax.sharding import PartitionSpec as P

STEPS_DEV = 4
SWEEPS = 4
COARSE_SWEEPS = 2


DIFFUSION = 0.5
DRIFT_X = 0.5
DRIFT_Y = 0.3
DRIFT_Z = 0.2


def extended(cells, sides, width):
    for axis, dim in sides:
        count = lax.axis_size(axis)
        ends = count - 1
        head = lax.slice_in_dim(cells, 0, width, axis=dim)
        tail = lax.slice_in_dim(cells, cells.shape[dim] - width, cells.shape[dim], axis=dim)
        cells = jnp.concatenate(
            [
                lax.ppermute(tail, axis, [(i, (i + 1) % count) for i in range(ends)]),
                cells,
                lax.ppermute(head, axis, [((i + 1) % count, i) for i in range(ends)]),
            ],
            axis=dim,
        )
    return cells


def shifted(value, axis, steps):
    count = lax.axis_size(axis)
    leading, last = (max(0, -steps), min(count, count - steps))
    return lax.ppermute(value, axis, [(source, source + steps) for source in range(leading, last)])


def relax(first, rhs, absorb, scale, sweeps):
    coupling = DIFFUSION * scale
    lean_x = DRIFT_X * scale
    lean_y = DRIFT_Y * scale
    lean_z = DRIFT_Z * scale
    diag = 1.0 + 6.0 * coupling + lean_x + lean_y + lean_z + scale * absorb
    value = first
    for sweep in range(sweeps):
        padded = extended(value, (("sx", 0), ("sy", 1)), 1)
        padded = jnp.pad(padded, ((0, 0), (0, 0), (1, 1)))
        low_x = padded[:-2, 1:-1, 1:-1]
        low_y = padded[1:-1, :-2, 1:-1]
        low_z = padded[1:-1, 1:-1, :-2]
        beside_all = low_x + padded[2:, 1:-1, 1:-1] + low_y + padded[1:-1, 2:, 1:-1]
        beside_all = beside_all + low_z + padded[1:-1, 1:-1, 2:]
        value = (
            rhs + coupling * beside_all + lean_x * low_x + lean_y * low_y + lean_z * low_z
        ) / diag
    return value


def advance(value, source, absorb):
    return relax(value, value + source, absorb, 1.0, SWEEPS)


def coarse_step(value, absorb):
    return relax(value, value, absorb, float(STEPS_DEV), COARSE_SWEEPS)


def on_device(start, guess, forcing, absorb):
    position = lax.axis_index("tm")
    count = lax.axis_size("tm")
    leading = position == 0
    own = guess[0]
    before = shifted(own, "tm", 1)
    state = jnp.where(leading, start, before)
    for inner in range(STEPS_DEV - 1):
        state = advance(state, forcing[inner], absorb)
    resid = advance(state, forcing[STEPS_DEV - 1], absorb) - own
    blank = jnp.zeros_like(resid)

    def turn(index, carry):
        received = shifted(carry, "tm", 1)
        return coarse_step(received, absorb) + resid

    error = lax.fori_loop(0, count, turn, blank)
    corrected = own + error
    before = shifted(corrected, "tm", 1)
    state = jnp.where(leading, start, before)
    pieces = []
    for inner in range(STEPS_DEV - 1):
        state = advance(state, forcing[inner], absorb)
        pieces.append(state)
    pieces.append(corrected)
    return jnp.stack(pieces, axis=0)


def solution(mesh):
    placed = (
        P("sx", "sy", None),
        P("tm", "sx", "sy", None),
        P("tm", "sx", "sy", None),
        P("sx", "sy", None),
    )
    return jax.shard_map(
        on_device, mesh=mesh, in_specs=placed, out_specs=P("tm", "sx", "sy", None), check_vma=False
    )
```

profile of v0, /device:TPU:65, one launch (start us, length us, event | category | flops | bytes accessed | tf_op | source)
XLA Modules:
  0.0 1221.3 jit_solution(14675874659941021263)
XLA Ops:
  3.2 9.1 collective-permute-done.9
  12.4 10.2 collective-permute-start.10
  267.8 745.9 %while.13 = (s32[]{:T(128)}, f32[8,32,256]{2,1,0:T(8,128)S(1)}, f32[8,32,256]{2,1,0:T(8,128)S(1)}, f32[8,32,256]{2,1,0:T(8,128)S(1)}, s32[]{:T(128)}, /*index=5*/s32[]{:T(128)}) while((s32[]{:T(128)}, f32[8,32,256]{2,1,0:T(8,128)S(1)}, f32[8,32,256]{2,1,0:T(8,128)S(1)}, f32[8,32,256]{2,1,0:T(8,128)S(1)}, s32[]{:T(128)}, ...), condition=%wide.region_1.2_spmd.clone, body=%wide.region_0.1_spmd.clone.sunk | while | flops 4779299 | bytes 8611575 | solution.py:85
  269.7 10.9 collective-permute-done
  280.6 6.5 collective-permute-start.1
  306.9 4.2 collective-permute-start.8
  314.5 11.2 collective-permute-done
  325.8 7.9 collective-permute-start.1
  340.3 4.2 collective-permute-start.4
  353.9 4.2 collective-permute-start.8
  361.5 11.2 collective-permute-done
  372.7 7.8 collective-permute-start.1
  387.0 4.2 collective-permute-start.4
  400.6 4.2 collective-permute-start.8
  408.2 11.2 collective-permute-done
  419.4 7.8 collective-permute-start.1
  433.8 4.2 collective-permute-start.4
  454.9 11.2 collective-permute-done
  466.2 7.8 collective-permute-start.1
  480.5 4.2 collective-permute-start.4
  494.0 4.2 collective-permute-start.8
  501.6 11.2 collective-permute-done
  512.9 7.8 collective-permute-start.1
  527.2 4.2 collective-permute-start.4
  548.4 11.2 collective-permute-done
  559.6 7.8 collective-permute-start.1
  573.9 4.2 collective-permute-start.4
  587.5 4.2 collective-permute-start.8
  595.1 11.2 collective-permute-done
  606.3 7.8 collective-permute-start.1
  641.8 11.2 collective-permute-done
  653.1 7.8 collective-permute-start.1
  688.6 11.2 collective-permute-done
  699.8 7.8 collective-permute-start.1
  735.3 11.2 collective-permute-done
  746.5 7.8 collective-permute-start.1
  782.0 11.2 collective-permute-done
  793.3 7.8 collective-permute-start.1
  828.8 11.2 collective-permute-done
  840.0 7.8 collective-permute-start.1
  875.5 11.2 collective-permute-done
  886.7 7.8 collective-permute-start.1
  922.2 11.2 collective-permute-done
  933.5 7.8 collective-permute-start.1
  968.9 11.2 collective-permute-done
  980.2 7.8 collective-permute-start.1
  1015.8 11.2 collective-permute-done.74
  1027.1 7.8 collective-permute-start.75
  (786 shorter events, 828.9 us)
Async XLA Ops:
  0.0 12.3 %collective-permute-start.9 = (f32[8,32,256]{2,1,0:T(8,128)}, f32[8,32,256]{2,1,0:T(8,128)S(1)}, u32[]{:S(2)}, u32[]{:S(2)}) collective-permute-start(f32[8,32,256]{2,1,0:T(8,128)} %bitcast.77), channel_id=1, source_target_pairs={{0,16},{16,32},{32,48},{48,64},{64,80},{80,96},{96,112},{112,128},... | collective-permute-start | bytes 786440 | tf_op jit(solution)/shard_map/ppermute | solution.py:37
  12.4 12.1 collective-permute-start.10
  267.8 12.8 %collective-permute-start = (f32[8,32,256]{2,1,0:T(8,128)S(1)}, f32[8,32,256]{2,1,0:T(8,128)S(1)}, u32[]{:S(2)}, u32[]{:S(2)}) collective-permute-start(f32[8,32,256]{2,1,0:T(8,128)S(1)} %broadcast_select_fusion.4), channel_id=1, source_target_pairs={{0,16},{16,32},{32,48},{48,64},{64,80},{80,96},{96,112},{112,128},... | collective-permute-start | bytes 786440 | tf_op jit(solution)/shard_map/while/body/eval_jaxpr/ppermute | solution.py:37
  280.6 8.4 collective-permute-start.1
  299.0 5.6 collective-permute-start.5
  312.6 13.2 %collective-permute-start = (f32[8,32,256]{2,1,0:T(8,128)S(1)}, f32[8,32,256]{2,1,0:T(8,128)S(1)}, u32[]{:S(2)}, u32[]{:S(2)}) collective-permute-start(f32[8,32,256]{2,1,0:T(8,128)S(1)} %broadcast_select_fusion.4), channel_id=1, source_target_pairs={{0,16},{16,32},{32,48},{48,64},{64,80},{80,96},{96,112},{112,128},... | collective-permute-start | bytes 786440 | tf_op jit(solution)/shard_map/while/body/eval_jaxpr/ppermute | solution.py:37
  325.8 9.9 collective-permute-start.1
  359.5 13.2 %collective-permute-start = (f32[8,32,256]{2,1,0:T(8,128)S(1)}, f32[8,32,256]{2,1,0:T(8,128)S(1)}, u32[]{:S(2)}, u32[]{:S(2)}) collective-permute-start(f32[8,32,256]{2,1,0:T(8,128)S(1)} %broadcast_select_fusion.4), channel_id=1, source_target_pairs={{0,16},{16,32},{32,48},{48,64},{64,80},{80,96},{96,112},{112,128},... | collective-permute-start | bytes 786440 | tf_op jit(solution)/shard_map/while/body/eval_jaxpr/ppermute | solution.py:37
  372.7 9.7 collective-permute-start.1
  406.3 13.2 %collective-permute-start = (f32[8,32,256]{2,1,0:T(8,128)S(1)}, f32[8,32,256]{2,1,0:T(8,128)S(1)}, u32[]{:S(2)}, u32[]{:S(2)}) collective-permute-start(f32[8,32,256]{2,1,0:T(8,128)S(1)} %broadcast_select_fusion.4), channel_id=1, source_target_pairs={{0,16},{16,32},{32,48},{48,64},{64,80},{80,96},{96,112},{112,128},... | collective-permute-start | bytes 786440 | tf_op jit(solution)/shard_map/while/body/eval_jaxpr/ppermute | solution.py:37
  419.4 9.7 collective-permute-start.1
  453.0 13.2 %collective-permute-start = (f32[8,32,256]{2,1,0:T(8,128)S(1)}, f32[8,32,256]{2,1,0:T(8,128)S(1)}, u32[]{:S(2)}, u32[]{:S(2)}) collective-permute-start(f32[8,32,256]{2,1,0:T(8,128)S(1)} %broadcast_select_fusion.4), channel_id=1, source_target_pairs={{0,16},{16,32},{32,48},{48,64},{64,80},{80,96},{96,112},{112,128},... | collective-permute-start | bytes 786440 | tf_op jit(solution)/shard_map/while/body/eval_jaxpr/ppermute | solution.py:37
  466.2 9.7 collective-permute-start.1
  486.1 5.6 collective-permute-start.5
  499.7 13.2 %collective-permute-start = (f32[8,32,256]{2,1,0:T(8,128)S(1)}, f32[8,32,256]{2,1,0:T(8,128)S(1)}, u32[]{:S(2)}, u32[]{:S(2)}) collective-permute-start(f32[8,32,256]{2,1,0:T(8,128)S(1)} %broadcast_select_fusion.4), channel_id=1, source_target_pairs={{0,16},{16,32},{32,48},{48,64},{64,80},{80,96},{96,112},{112,128},... | collective-permute-start | bytes 786440 | tf_op jit(solution)/shard_map/while/body/eval_jaxpr/ppermute | solution.py:37
  512.9 9.7 collective-permute-start.1
  546.4 13.2 %collective-permute-start = (f32[8,32,256]{2,1,0:T(8,128)S(1)}, f32[8,32,256]{2,1,0:T(8,128)S(1)}, u32[]{:S(2)}, u32[]{:S(2)}) collective-permute-start(f32[8,32,256]{2,1,0:T(8,128)S(1)} %broadcast_select_fusion.4), channel_id=1, source_target_pairs={{0,16},{16,32},{32,48},{48,64},{64,80},{80,96},{96,112},{112,128},... | collective-permute-start | bytes 786440 | tf_op jit(solution)/shard_map/while/body/eval_jaxpr/ppermute | solution.py:37
  559.6 9.7 collective-permute-start.1
  579.6 5.6 collective-permute-start.5
  593.2 13.2 %collective-permute-start = (f32[8,32,256]{2,1,0:T(8,128)S(1)}, f32[8,32,256]{2,1,0:T(8,128)S(1)}, u32[]{:S(2)}, u32[]{:S(2)}) collective-permute-start(f32[8,32,256]{2,1,0:T(8,128)S(1)} %broadcast_select_fusion.4), channel_id=1, source_target_pairs={{0,16},{16,32},{32,48},{48,64},{64,80},{80,96},{96,112},{112,128},... | collective-permute-start | bytes 786440 | tf_op jit(solution)/shard_map/while/body/eval_jaxpr/ppermute | solution.py:37
  606.3 9.7 collective-permute-start.1
  626.3 5.6 collective-permute-start.5
  639.9 13.2 %collective-permute-start = (f32[8,32,256]{2,1,0:T(8,128)S(1)}, f32[8,32,256]{2,1,0:T(8,128)S(1)}, u32[]{:S(2)}, u32[]{:S(2)}) collective-permute-start(f32[8,32,256]{2,1,0:T(8,128)S(1)} %broadcast_select_fusion.4), channel_id=1, source_target_pairs={{0,16},{16,32},{32,48},{48,64},{64,80},{80,96},{96,112},{112,128},... | collective-permute-start | bytes 786440 | tf_op jit(solution)/shard_map/while/body/eval_jaxpr/ppermute | solution.py:37
  653.1 9.7 collective-permute-start.1
  673.1 5.6 collective-permute-start.5
  686.6 13.2 %collective-permute-start = (f32[8,32,256]{2,1,0:T(8,128)S(1)}, f32[8,32,256]{2,1,0:T(8,128)S(1)}, u32[]{:S(2)}, u32[]{:S(2)}) collective-permute-start(f32[8,32,256]{2,1,0:T(8,128)S(1)} %broadcast_select_fusion.4), channel_id=1, source_target_pairs={{0,16},{16,32},{32,48},{48,64},{64,80},{80,96},{96,112},{112,128},... | collective-permute-start | bytes 786440 | tf_op jit(solution)/shard_map/while/body/eval_jaxpr/ppermute | solution.py:37
  699.8 9.7 collective-permute-start.1
  719.8 5.6 collective-permute-start.5
  733.4 13.2 %collective-permute-start = (f32[8,32,256]{2,1,0:T(8,128)S(1)}, f32[8,32,256]{2,1,0:T(8,128)S(1)}, u32[]{:S(2)}, u32[]{:S(2)}) collective-permute-start(f32[8,32,256]{2,1,0:T(8,128)S(1)} %broadcast_select_fusion.4), channel_id=1, source_target_pairs={{0,16},{16,32},{32,48},{48,64},{64,80},{80,96},{96,112},{112,128},... | collective-permute-start | bytes 786440 | tf_op jit(solution)/shard_map/while/body/eval_jaxpr/ppermute | solution.py:37
  746.5 9.7 collective-permute-start.1
  766.5 5.6 collective-permute-start.5
  780.1 13.2 %collective-permute-start = (f32[8,32,256]{2,1,0:T(8,128)S(1)}, f32[8,32,256]{2,1,0:T(8,128)S(1)}, u32[]{:S(2)}, u32[]{:S(2)}) collective-permute-start(f32[8,32,256]{2,1,0:T(8,128)S(1)} %broadcast_select_fusion.4), channel_id=1, source_target_pairs={{0,16},{16,32},{32,48},{48,64},{64,80},{80,96},{96,112},{112,128},... | collective-permute-start | bytes 786440 | tf_op jit(solution)/shard_map/while/body/eval_jaxpr/ppermute | solution.py:37
  793.3 9.7 collective-permute-start.1
  813.2 5.6 collective-permute-start.5
  826.8 13.2 %collective-permute-start = (f32[8,32,256]{2,1,0:T(8,128)S(1)}, f32[8,32,256]{2,1,0:T(8,128)S(1)}, u32[]{:S(2)}, u32[]{:S(2)}) collective-permute-start(f32[8,32,256]{2,1,0:T(8,128)S(1)} %broadcast_select_fusion.4), channel_id=1, source_target_pairs={{0,16},{16,32},{32,48},{48,64},{64,80},{80,96},{96,112},{112,128},... | collective-permute-start | bytes 786440 | tf_op jit(solution)/shard_map/while/body/eval_jaxpr/ppermute | solution.py:37
  840.0 9.7 collective-permute-start.1
  860.0 5.6 collective-permute-start.5
  873.6 13.2 %collective-permute-start = (f32[8,32,256]{2,1,0:T(8,128)S(1)}, f32[8,32,256]{2,1,0:T(8,128)S(1)}, u32[]{:S(2)}, u32[]{:S(2)}) collective-permute-start(f32[8,32,256]{2,1,0:T(8,128)S(1)} %broadcast_select_fusion.4), channel_id=1, source_target_pairs={{0,16},{16,32},{32,48},{48,64},{64,80},{80,96},{96,112},{112,128},... | collective-permute-start | bytes 786440 | tf_op jit(solution)/shard_map/while/body/eval_jaxpr/ppermute | solution.py:37
  886.7 9.7 collective-permute-start.1
  906.7 5.6 collective-permute-start.5
  920.3 13.2 %collective-permute-start = (f32[8,32,256]{2,1,0:T(8,128)S(1)}, f32[8,32,256]{2,1,0:T(8,128)S(1)}, u32[]{:S(2)}, u32[]{:S(2)}) collective-permute-start(f32[8,32,256]{2,1,0:T(8,128)S(1)} %broadcast_select_fusion.4), channel_id=1, source_target_pairs={{0,16},{16,32},{32,48},{48,64},{64,80},{80,96},{96,112},{112,128},... | collective-permute-start | bytes 786440 | tf_op jit(solution)/shard_map/while/body/eval_jaxpr/ppermute | solution.py:37
  933.5 9.7 collective-permute-start.1
  953.4 5.6 collective-permute-start.5
  967.0 13.2 %collective-permute-start = (f32[8,32,256]{2,1,0:T(8,128)S(1)}, f32[8,32,256]{2,1,0:T(8,128)S(1)}, u32[]{:S(2)}, u32[]{:S(2)}) collective-permute-start(f32[8,32,256]{2,1,0:T(8,128)S(1)} %broadcast_select_fusion.4), channel_id=1, source_target_pairs={{0,16},{16,32},{32,48},{48,64},{64,80},{80,96},{96,112},{112,128},... | collective-permute-start | bytes 786440 | tf_op jit(solution)/shard_map/while/body/eval_jaxpr/ppermute | solution.py:37
  980.2 9.7 collective-permute-start.1
  1000.2 5.6 collective-permute-start.5
  1013.8 13.3 %collective-permute-start.74 = (f32[8,32,256]{2,1,0:T(8,128)S(1)}, f32[8,32,256]{2,1,0:T(8,128)S(1)}, u32[]{:S(2)}, u32[]{:S(2)}) collective-permute-start(f32[8,32,256]{2,1,0:T(8,128)S(1)} %bitcast_add_fusion.7), channel_id=1, source_target_pairs={{0,16},{16,32},{32,48},{48,64},{64,80},{80,96},{96,112},{112,128},... | collective-permute-start | bytes 786440 | tf_op jit(solution)/shard_map/ppermute | solution.py:37
  1027.1 9.7 collective-permute-start.75
  (214 other events, 1074.1 us)
where the time goes:
time: 1230 us; the launch traced here: 1220 us
  starting transfers between devices  706 us (57%)
  waiting for transfers between devices  472 us (38%)
  other arithmetic  36.7 us (3%)
    ppermute x120, starting transfers between devices, extended(): lax.ppermute(tail, axis, [(i, (i + 1) % count) for i in range(ends)])  477 us
    ppermute x120, waiting for transfers between devices, extended(): lax.ppermute(head, axis, [((i + 1) % count, i) for i in range(ends)])  231 us
    ppermute x18, waiting for transfers between devices, shifted(): lax.ppermute(value, axis, [(source, source + steps) for source in range(l...  200 us
    ppermute x120, starting transfers between devices, extended(): lax.ppermute(head, axis, [((i + 1) % count, i) for i in range(ends)])  193 us
    ppermute x120, waiting for transfers between devices, extended(): lax.ppermute(tail, axis, [(i, (i + 1) % count) for i in range(ends)])  41.1 us
    ppermute x18, starting transfers between devices, shifted(): lax.ppermute(value, axis, [(source, source + steps) for source in range(l...  36 us
  transfers between devices with their start and end apart: 258, of which 138 were waited for; matrix products, arithmetic and copies ran while one was open for 0% of the time, Pallas kernels for 0%

commit v1 on v0

v1 whole, which is shorter than its diff:
```python
import functools
import jax
import jax.numpy as jnp
from jax import lax
from jax.experimental import pallas as pl
from jax.experimental.pallas import tpu as pltpu
from jax.sharding import PartitionSpec as P

NX = 32
ROWS = 8
NZ = 256
EXT = 3 * ROWS
PART = 64
MARGIN = 32
WINDOW = PART + 2 * MARGIN
GROUP = 4
F32 = jnp.float32
WX = 2.0
WY = 1.6
WZ = 1.4


def device_of(block):
    sy, local = divmod(block % 16, 4)
    return (local ^ (2 * (sy & 1))) * 4 + sy


def block_swap(first):
    pairs = []
    for block in range(16):
        other = block + 1 if (block - first) % 2 == 0 else block - 1
        pairs.append((device_of(block), device_of(other % 16)))
    return pairs


IN_CHIP = block_swap(0)
OFF_CHIP = block_swap(1)


def both_sides(value):
    axes = ("sx", "sy")
    return lax.ppermute(value, axes, IN_CHIP), lax.ppermute(value, axes, OFF_CHIP)


def sweep(source, target, hinv, rhs, closed):
    width = source.shape[2]
    rows = source.shape[1]
    lane = lax.broadcasted_iota(jnp.int32, (rows, width), 1)

    def body(x, carry):
        here = source[x + 1]
        low_z = pltpu.roll(here, 1, 1)
        high_z = pltpu.roll(here, width - 1, 1)
        if closed:
            low_z = jnp.where(lane == 0, 0.0, low_z)
            high_z = jnp.where(lane == width - 1, 0.0, high_z)
        low_y = pltpu.roll(here, 1, 0)
        high_y = pltpu.roll(here, rows - 1, 0)
        total = (source[x + 2] + WX * source[x]) + (high_y + WY * low_y) + (high_z + WZ * low_z)
        target[x + 1] = (total + rhs(x, here)) * hinv[x]
        return carry

    lax.fori_loop(0, NX, body, 0, unroll=4)


def clear_ends(*states):
    for state in states:
        blank = jnp.zeros(state.shape[1:], F32)
        state[0] = blank
        state[NX + 1] = blank


def joined(flags, centre, in_chip, off_chip):
    low = in_chip * flags[0] + off_chip * flags[1]
    high = in_chip * flags[2] + off_chip * flags[3]
    return jnp.concatenate([low, centre, high], axis=0)


def each_x(body):
    def step(x, carry):
        body(x)
        return carry

    lax.fori_loop(0, NX, step, 0, unroll=2)


def relax(a, b, hinv, saved, sweeps, closed, scale, extra=None):
    def first(x, here):
        value = scale * here if extra is None else scale * (here + extra(x))
        saved[x] = value
        return value

    sweep(a, b, hinv, first, closed)
    for index in range(1, sweeps):
        source, target = (b, a) if index % 2 else (a, b)
        sweep(source, target, hinv, lambda x, here: saved[x], closed)


def centre_of(value):
    return value[ROWS : 2 * ROWS]


def begin_kernel(flags, x_c, x_i, x_o, s_c, s_i, s_o, place, w1, w2, fine, coarse, window, a, b, saved):
    fl = [flags[k] for k in range(4)]
    shift = place[0]
    lane = lax.broadcasted_iota(jnp.int32, (EXT, WINDOW), 1) + place[1]
    inside = jnp.logical_and(lane >= 0, lane < NZ)
    row = lax.broadcasted_iota(jnp.int32, (EXT, NZ), 0) + place[2]
    real = jnp.logical_and(row >= 0, row < 16 * ROWS)
    clear_ends(a, b)

    def fill(x):
        hi, lo = x // 8, x % 8
        a[x + 1] = joined(fl, x_c[x], x_i[x], x_o[x])
        absorb = joined(fl, s_c[hi, 0, lo], s_i[hi, 0, lo], s_o[hi, 0, lo])
        fine[x] = jnp.where(real, 0.5 / (5.0 + absorb), 0.0)
        value = jnp.where(real, 2.0 / (17.0 + 4.0 * absorb), 0.0)
        coarse[x] = value
        window[x] = jnp.where(inside, pltpu.roll(value, shift, 1)[:, :WINDOW], 0.0)

    each_x(fill)

    def source(index):
        def get(x):
            hi, lo = x // 8, x % 8
            return joined(fl, s_c[hi, index, lo], s_i[hi, index, lo], s_o[hi, index, lo])

        return get

    for index, out in ((1, w1), (2, w2)):
        relax(a, b, fine, saved, 4, True, 2.0, source(index))

        def put(x):
            out[x] = centre_of(a[x + 1])

        each_x(put)


def resid_kernel(flags, v_c, v_i, v_o, s_c, s_i, s_o, own, fine, w3, resid, chunks, a, b, saved):
    fl = [flags[k] for k in range(4)]
    clear_ends(a, b)

    def fill(x):
        a[x + 1] = joined(fl, v_c[x], v_i[x], v_o[x])

    each_x(fill)

    def source(index):
        def get(x):
            hi, lo = x // 8, x % 8
            return joined(fl, s_c[hi, index, lo], s_i[hi, index, lo], s_o[hi, index, lo])

        return get

    relax(a, b, fine, saved, 4, True, 2.0, source(0))

    def put(x):
        w3[x] = centre_of(a[x + 1])

    each_x(put)
    relax(a, b, fine, saved, 4, True, 2.0, source(1))
    lane = lax.broadcasted_iota(jnp.int32, (ROWS, WINDOW), 1)

    def split(x):
        value = centre_of(a[x + 1]) - own[x // 8, x % 8]
        resid[x] = value
        for part in range(GROUP):
            start = PART * part - MARGIN
            turned = pltpu.roll(value, (-start) % NZ, 1)[:, :WINDOW]
            if part == 0:
                turned = jnp.where(lane < MARGIN, 0.0, turned)
            if part == GROUP - 1:
                turned = jnp.where(lane >= WINDOW - MARGIN, 0.0, turned)
            chunks[part, x] = turned

    each_x(split)


def chain_kernel(first, last, flags, r_c, r_i, r_o, hinv, *refs):
    if first:
        out, a, b, saved = refs
    else:
        e_c, e_i, e_o, out, a, b, saved = refs
    fl = [flags[k] for k in range(4)]
    clear_ends(a, b)
    lane = lax.broadcasted_iota(jnp.int32, (ROWS, WINDOW), 1)

    def added(step, x):
        if step < GROUP - 1:
            return joined(fl, r_c[step, x], r_i[step, x], r_o[step, x])
        blank = jnp.zeros((ROWS, WINDOW), F32)
        return jnp.concatenate([blank, r_c[step, x], blank], axis=0)

    def fill(x):
        if first:
            a[x + 1] = added(0, x)
        else:
            gate = flags[4]
            a[x + 1] = gate * joined(fl, e_c[x], e_i[x], e_o[x])

    each_x(fill)

    def pack(step):
        def put(x, carry):
            low = pltpu.roll(centre_of(a[x + 1]), WINDOW - MARGIN, 1)
            high = pltpu.roll(centre_of(a[x + 1 + NX // 2]), MARGIN, 1)
            out[step, x] = jnp.where(lane < PART, low, high)
            return carry

        lax.fori_loop(0, NX // 2, put, 0, unroll=2)

    for step in range(1 if first else 0, GROUP):
        if last:
            pack(step)
            if step == GROUP - 1:
                return
        relax(a, b, hinv, saved, 2, False, 0.5)

        def add(x):
            a[x + 1] = a[x + 1] + added(step, x)

        each_x(add)

    def put_all(x):
        out[x] = centre_of(a[x + 1])

    each_x(put_all)


def unpacked(packed, x, lane):
    p = [packed[part, x] for part in range(GROUP)]
    low = lane < PART
    first = jnp.concatenate(
        [jnp.where(low, p[0], pltpu.roll(p[1], PART, 1)), jnp.where(low, p[2], pltpu.roll(p[3], PART, 1))],
        axis=1,
    )
    second = jnp.concatenate(
        [jnp.where(low, pltpu.roll(p[0], PART, 1), p[1]), jnp.where(low, pltpu.roll(p[2], PART, 1), p[3])],
        axis=1,
    )
    return first, second


def correct_kernel(
    flags, d_c, d_i, d_o, fine, coarse, own, resid, w1, w2, out, y2, a, b, saved, kept
):
    fl = [flags[k] for k in range(4)]
    clear_ends(a, b)
    lane = lax.broadcasted_iota(jnp.int32, (ROWS, WINDOW), 1)
    half = NX // 2

    def fill(x, carry):
        for index, values in enumerate(
            zip(unpacked(d_c, x, lane), unpacked(d_i, x, lane), unpacked(d_o, x, lane))
        ):
            value = joined(fl, *values)
            a[x + half * index + 1] = value
            kept[x + half * index] = value
        return carry

    lax.fori_loop(0, half, fill, 0)
    relax(a, b, coarse, saved, 2, True, 0.5)

    def put(x):
        hi, lo = x // 8, x % 8
        out[hi, 2, lo] = (centre_of(a[x + 1]) + resid[x]) + own[hi, lo]
        a[x + 1] = kept[x]

    each_x(put)
    for index, base in enumerate((w1, w2)):
        relax(a, b, fine, saved, 4, True, 2.0)

        def place(x):
            value = centre_of(a[x + 1])
            out[x // 8, index, x % 8] = value + base[x]
            if index == 1:
                y2[x] = value

        each_x(place)


def end_kernel(flags, y_c, y_i, y_o, fine, w3, out, a, b, saved):
    fl = [flags[k] for k in range(4)]
    clear_ends(a, b)

    def fill(x):
        a[x + 1] = joined(fl, y_c[x], y_i[x], y_o[x])

    each_x(fill)
    relax(a, b, fine, saved, 4, True, 2.0)

    def put(x):
        out[x // 8, x % 8] = centre_of(a[x + 1]) + w3[x]

    each_x(put)


def call(kernel, outs, width, args, smem, kept=False):
    scratch = [
        pltpu.VMEM((NX + 2, EXT, width), F32),
        pltpu.VMEM((NX + 2, EXT, width), F32),
        pltpu.VMEM((NX, EXT, width), F32),
    ]
    if kept:
        scratch.append(pltpu.VMEM((NX, EXT, width), F32))
    specs = [
        pl.BlockSpec(memory_space=pltpu.SMEM if index in smem else pltpu.VMEM)
        for index in range(len(args))
    ]
    return pl.pallas_call(
        kernel,
        out_shape=[jax.ShapeDtypeStruct(shape, F32) for shape in outs],
        in_specs=specs,
        out_specs=[pl.BlockSpec(memory_space=pltpu.VMEM)] * len(outs),
        scratch_shapes=scratch,
        compiler_params=pltpu.CompilerParams(vmem_limit_bytes=48 * 2**20),
    )(*args)


def on_device(start, guess, forcing, absorb):
    tm = lax.axis_index("tm")
    sx = lax.axis_index("sx")
    sy = lax.axis_index("sy")
    turned = sy % 2 == 1
    local = jnp.where(turned, (sx + 2) % 4, sx)
    block = 4 * sy + local
    even = block % 2 == 0
    inner_low = jnp.logical_not(even)
    outer_low = jnp.logical_and(even, block > 0)
    inner_high = even
    outer_high = jnp.logical_and(jnp.logical_not(even), block < 15)
    gate = tm >= GROUP
    flags = jnp.stack([inner_low, outer_low, inner_high, outer_high, gate]).astype(F32)
    part = tm % GROUP
    place = jnp.stack([(MARGIN - PART * part) % NZ, PART * part - MARGIN, ROWS * block - ROWS])
    place = place.astype(jnp.int32)

    def to_blocks(fields):
        count = fields.shape[0]
        cut = fields.reshape(count, 8, 4, ROWS, NZ)
        cut = jnp.where(turned, jnp.roll(cut, 2, axis=2), cut)
        return lax.all_to_all(jnp.moveaxis(cut, 2, 0), "sx", 0, 0)

    own = guess[0]
    shifted = lax.ppermute(own, "tm", [(c, (c + 1) % 16) for c in range(16)])
    early = to_blocks(jnp.stack([absorb, forcing[0], forcing[1]]))
    early_i, early_o = both_sides(early)
    before = to_blocks(jnp.where(tm == 0, start, shifted)[None]).reshape(NX, ROWS, NZ)
    before_i, before_o = both_sides(before)
    late = to_blocks(jnp.concatenate([forcing[2:4], guess], axis=0))
    late_f = late[:, :2]
    late_i, late_o = both_sides(late_f)
    guess_b = late[:, 2]

    field = (NX, ROWS, NZ)
    w1, w2, fine, coarse, window = call(
        begin_kernel,
        [field, field, (NX, EXT, NZ), (NX, EXT, NZ), (NX, EXT, WINDOW)],
        NZ,
        (flags, before, before_i, before_o, early, early_i, early_o, place),
        (0, 7),
    )
    w2_i, w2_o = both_sides(w2)
    w3, resid, chunks = call(
        resid_kernel,
        [field, field, (GROUP, NX, ROWS, WINDOW)],
        NZ,
        (flags, w2, w2_i, w2_o, late_f, late_i, late_o, guess_b, fine),
        (0,),
    )
    groups = [[GROUP * g + j for j in range(GROUP)] for g in range(4)]
    held = lax.all_to_all(chunks, "tm", 0, 0, axis_index_groups=groups)
    held_i, held_o = both_sides(held[: GROUP - 1])
    plane = (NX, ROWS, WINDOW)
    (state,) = call(
        functools.partial(chain_kernel, True, False), [plane], WINDOW,
        (flags, held, held_i, held_o, window), (0,),
    )
    for turn in range(3):
        state = lax.ppermute(state, "tm", [(c, (c + GROUP) % 16) for c in range(16)])
        state_i, state_o = both_sides(state)
        last = turn == 2
        (state,) = call(
            functools.partial(chain_kernel, False, last),
            [(GROUP, NX // 2, ROWS, WINDOW) if last else plane], WINDOW,
            (flags, held, held_i, held_o, window, state, state_i, state_o), (0,),
        )
    error = lax.all_to_all(state, "tm", 0, 0, axis_index_groups=groups)
    error_i, error_o = both_sides(error)
    out, y2 = call(
        correct_kernel,
        [(4, 3, 8, ROWS, NZ), field],
        NZ,
        (flags, error, error_i, error_o, fine, coarse, guess_b, resid, w1, w2),
        (0,),
        kept=True,
    )
    y2_i, y2_o = both_sides(y2)
    (last,) = call(
        end_kernel, [(4, 8, ROWS, NZ)], NZ, (flags, y2, y2_i, y2_o, fine, w3), (0,)
    )
    fields = jnp.stack([out[:, 0], out[:, 1], last, out[:, 2]], axis=1)
    back = lax.all_to_all(fields, "sx", 0, 0)
    back = jnp.where(turned, jnp.roll(back, 2, axis=0), back)
    return jnp.moveaxis(back, 0, 2).reshape(4, 8, 4 * ROWS, NZ)


def solution(mesh):
    placed = (
        P("sx", "sy", None),
        P("tm", "sx", "sy", None),
        P("tm", "sx", "sy", None),
        P("sx", "sy", None),
    )
    return jax.shard_map(
        on_device, mesh=mesh, in_specs=placed, out_specs=P("tm", "sx", "sy", None), check_vma=False
    )
```

time: 1230 us -> 258 us (0.21)
  the two profiles are of different devices: /device:TPU:65 before, /device:TPU:1 now
where the time goes in v1:
time: 258 us; the launch traced here: 257 us
  waiting for transfers between devices  97.3 us (38%)
  Pallas kernels  68.2 us (26%)
  starting transfers between devices  46.5 us (18%)
  blocking collectives  35.1 us (14%)
  local copies, waits for them, and re-layouts  6.93 us (3%)
  other arithmetic  2.64 us (1%)
    pallas_call x8, Pallas kernels, call(): pl.pallas_call(kernel, out_shape=[jax.ShapeDtypeStruct(shape, F32) for sh...  68.2 us
    ppermute x10, waiting for transfers between devices, both_sides(): lax.ppermute(value, axes, OFF_CHIP)  37.8 us
    ppermute x10, starting transfers between devices, both_sides(): lax.ppermute(value, axes, IN_CHIP)  21.8 us
    all_to_all x3, waiting for transfers between devices, to_blocks(): return lax.all_to_all(jnp.moveaxis(cut, 2, 0), 'sx', 0, 0)  20 us
    ppermute x3, waiting for transfers between devices, on_device(): lax.ppermute(state, 'tm', [(c, (c + GROUP) % 16) for c in range(16)])  19.2 us
    all_to_all x3, starting transfers between devices, to_blocks(): return lax.all_to_all(jnp.moveaxis(cut, 2, 0), 'sx', 0, 0)  17 us
    all_to_all x1, blocking collectives, on_device(): back = lax.all_to_all(fields, 'sx', 0, 0)  16.9 us
    ppermute x1, waiting for transfers between devices, on_device(): shifted = lax.ppermute(own, 'tm', [(c, (c + 1) % 16) for c in range(16)])  15 us
  transfers between devices with their start and end apart: 27, of which 21 were waited for; matrix products, arithmetic and copies ran while one was open for 2% of the time, Pallas kernels for 4%

profile of v1, /device:TPU:1, one launch (start us, length us, event | category | flops | bytes accessed | tf_op | source)
XLA Modules:
  0.0 257.0 jit_solution(11097146442378494197)
XLA Ops:
  0.0 2.1 collective-permute-start
  2.1 15.0 %collective-permute-done = f32[8,32,256]{2,1,0:T(8,128)S(1)} collective-permute-done((f32[8,32,256]{2,1,0:T(8,128)}, f32[8,32,256]{2,1,0:T(8,128)S(1)}, u32[]{:S(2)}, u32[]{:S(2)}) %collective-permute-start) | collective-permute-done | bytes 262176 | tf_op jit(solution)/shard_map/ppermute | solution.py:345
  17.1 1.0 select_bitcast_fusion
  19.8 7.6 %all-to-all-start = ((f32[4,1,8,8,256]{4,3,2,1,0:T(8,128)}), f32[4,1,8,8,256]{4,3,2,1,0:T(8,128)S(1)}, u32[]{:S(2)}, u32[]{:S(2)}) async-start(f32[4,1,8,8,256]{4,3,2,1,0:T(8,128)} %copy.36), calls=%async_computation | async-start | bytes 524288 | tf_op jit(solution)/shard_map/all_to_all | solution.py:342
  29.5 3.0 %all-to-all-done = f32[4,1,8,8,256]{4,3,2,1,0:T(8,128)S(1)} async-done(((f32[4,1,8,8,256]{4,3,2,1,0:T(8,128)}), f32[4,1,8,8,256]{4,3,2,1,0:T(8,128)S(1)}, u32[]{:S(2)}, u32[]{:S(2)}) %all-to-all-start) | async-done | bytes 262176 | tf_op jit(solution)/shard_map/all_to_all | solution.py:342
  32.5 4.4 %all-to-all-start.1 = ((f32[4,3,8,8,256]{4,3,2,1,0:T(8,128)}), f32[4,3,8,8,256]{4,3,2,1,0:T(8,128)S(1)}, u32[]{:S(2)}, u32[]{:S(2)}) async-start(f32[4,3,8,8,256]{4,3,2,1,0:T(8,128)} %copy.37), calls=%async_computation.1 | async-start | bytes 1572864 | tf_op jit(solution)/shard_map/all_to_all | solution.py:342
  37.1 1.0 copy.38
  38.1 9.6 %all-to-all-done.1.s_c = f32[4,3,8,8,256]{4,3,2,1,0:T(8,128)S(1)} async-done(((f32[4,3,8,8,256]{4,3,2,1,0:T(8,128)}), f32[4,3,8,8,256]{4,3,2,1,0:T(8,128)S(1)}, u32[]{:S(2)}, u32[]{:S(2)}) %all-to-all-start.1) | async-done | bytes 786464 | tf_op jit(solution)/shard_map/all_to_all | solution.py:342
  47.7 5.0 %all-to-all-start.2 = ((f32[4,3,8,8,256]{4,3,2,1,0:T(8,128)}), f32[4,3,8,8,256]{4,3,2,1,0:T(8,128)}, u32[]{:S(2)}, u32[]{:S(2)}) async-start(f32[4,3,8,8,256]{4,3,2,1,0:T(8,128)} %copy.38), calls=%async_computation.2 | async-start | bytes 1572864 | tf_op jit(solution)/shard_map/all_to_all | solution.py:342
  52.8 1.6 collective-permute-start.4
  54.5 1.2 collective-permute-start.1
  56.1 7.5 %all-to-all-done.2 = f32[4,3,8,8,256]{4,3,2,1,0:T(8,128)} async-done(((f32[4,3,8,8,256]{4,3,2,1,0:T(8,128)}), f32[4,3,8,8,256]{4,3,2,1,0:T(8,128)}, u32[]{:S(2)}, u32[]{:S(2)}) %all-to-all-start.2) | async-done | bytes 786464 | tf_op jit(solution)/shard_map/all_to_all | solution.py:342
  63.6 1.1 slice.78.s_c
  66.1 9.2 %collective-permute-done.2.x_o = f32[32,8,256]{2,1,0:T(8,128)} collective-permute-done((f32[32,8,256]{2,1,0:T(8,128)S(1)}, f32[32,8,256]{2,1,0:T(8,128)}, u32[]{:S(2)}, u32[]{:S(2)}) %collective-permute-start.2) | collective-permute-done | bytes 262176 | tf_op jit(solution)/shard_map/ppermute | solution.py:42
  75.3 11.0 %shard_map.46 = (f32[32,8,256]{2,1,0:T(8,128)S(1)}, f32[32,8,256]{2,1,0:T(8,128)S(1)}, f32[32,24,256]{2,1,0:T(8,128)S(1)}, f32[32,24,256]{2,1,0:T(8,128)S(1)}, f32[32,24,128]{2,1,0:T(8,128)S(1)}) custom-call(f32[5]{0:T(128)S(1)} %convert_element_type.3.flags, f32[32,8,256]{2,1,0:T(8,128)S(1)} %bitcast.41, f32[32,8,256]{2,1,0:T(8,128)S(1)} %collective-permute-done.1.x_i, ...), custom_call_target="tpu_custom_call" | custom-call | tf_op jit(solution)/shard_map/pallas_call | solution.py:310
  87.9 4.7 %collective-permute-done.6.v_o = f32[32,8,256]{2,1,0:T(8,128)S(1)} collective-permute-done((f32[32,8,256]{2,1,0:T(8,128)S(1)}, f32[32,8,256]{2,1,0:T(8,128)S(1)}, u32[]{:S(2)}, u32[]{:S(2)}) %collective-permute-start.6) | collective-permute-done | bytes 262176 | tf_op jit(solution)/shard_map/ppermute | solution.py:42
  92.6 10.9 %shard_map.47 = (f32[32,8,256]{2,1,0:T(8,128)S(1)}, f32[32,8,256]{2,1,0:T(8,128)S(1)}, f32[4,32,8,128]{3,2,1,0:T(8,128)S(1)}) custom-call(f32[5]{0:T(128)S(1)} %convert_element_type.3.flags, f32[32,8,256]{2,1,0:T(8,128)S(1)} %get-tuple-element.15.v_c.w2, f32[32,8,256]{2,1,0:T(8,128)S(1)} %collective-permute-done.5.v_i, ...), custom_call_target="tpu_custom_call" | custom-call | tf_op jit(solution)/shard_map/pallas_call | solution.py:310
  103.5 10.3 %all_to_all.30.r_c = f32[4,32,8,128]{3,2,1,0:T(8,128)S(1)} all-to-all(f32[4,32,8,128]{3,2,1,0:T(8,128)S(1)} %get-tuple-element.17), channel_id=1, replica_groups={{0,16,32,48},{64,80,96,112},{128,144,160,176},{192,208,224,240},{1,17,3..., dimensions={0} | all-to-all | bytes 1048576 | tf_op jit(solution)/shard_map/all_to_all | solution.py:372
  113.8 2.6 %collective-permute-start.10 = (f32[3,32,8,128]{3,2,1,0:T(8,128)S(1)}, f32[3,32,8,128]{3,2,1,0:T(8,128)S(1)}, u32[]{:S(2)}, u32[]{:S(2)}) collective-permute-start(f32[3,32,8,128]{3,2,1,0:T(8,128)S(1)} %slice.80), channel_id=1, source_target_pairs={{0,7},{4,8},{8,4},{12,9},{9,12},{13,1},{1,13},{5,2},{2,5},{6,10},{... | collective-permute-start | bytes 1179656 | tf_op jit(solution)/shard_map/ppermute | solution.py:42
  116.4 2.8 %collective-permute-start.9 = (f32[3,32,8,128]{3,2,1,0:T(8,128)S(1)}, f32[3,32,8,128]{3,2,1,0:T(8,128)S(1)}, u32[]{:S(2)}, u32[]{:S(2)}) collective-permute-start(f32[3,32,8,128]{3,2,1,0:T(8,128)S(1)} %slice.80), channel_id=1, source_target_pairs={{0,4},{4,0},{8,12},{12,8},{9,13},{13,9},{1,5},{5,1},{2,6},{6,2},{1... | collective-permute-start | bytes 1179656 | tf_op jit(solution)/shard_map/ppermute | solution.py:42
  119.1 3.0 %collective-permute-done.10.r_o = f32[3,32,8,128]{3,2,1,0:T(8,128)S(1)} collective-permute-done((f32[3,32,8,128]{3,2,1,0:T(8,128)S(1)}, f32[3,32,8,128]{3,2,1,0:T(8,128)S(1)}, u32[]{:S(2)}, u32[]{:S(2)}) %collective-permute-start.10) | collective-permute-done | bytes 393248 | tf_op jit(solution)/shard_map/ppermute | solution.py:42
  122.1 5.7 %shard_map.48 = f32[32,8,128]{2,1,0:T(8,128)S(1)} custom-call(f32[5]{0:T(128)S(1)} %convert_element_type.3.flags, f32[4,32,8,128]{3,2,1,0:T(8,128)S(1)} %all_to_all.30.r_c, f32[3,32,8,128]{3,2,1,0:T(8,128)S(1)} %collective-permute-done.9.r_i, f32[3,32,8,128]{3,2,1,0:T(8,128)S(1)} %collective-permute-done.10.r_o, f32[32,24,128]{2,1,0:T(8,128)S(1)} %get-tuple-element.18.hinv), custom_call_target="tpu_custom_call" | custom-call | tf_op jit(solution)/shard_map/pallas_call | solution.py:310
  128.0 6.4 %collective-permute-done.11.refs_0_ = f32[32,8,128]{2,1,0:T(8,128)S(1)} collective-permute-done((f32[32,8,128]{2,1,0:T(8,128)S(1)}, f32[32,8,128]{2,1,0:T(8,128)S(1)}, u32[]{:S(2)}, u32[]{:S(2)}) %collective-permute-start.11) | collective-permute-done | bytes 131104 | tf_op jit(solution)/shard_map/ppermute | solution.py:380
  134.3 4.8 %collective-permute-start.12 = (f32[32,8,128]{2,1,0:T(8,128)S(1)}, f32[32,8,128]{2,1,0:T(8,128)S(1)}, u32[]{:S(2)}, u32[]{:S(2)}) collective-permute-start(f32[32,8,128]{2,1,0:T(8,128)S(1)} %collective-permute-done.11.refs_0_), channel_id=1, source_target_pairs={{0,4},{4,0},{8,12},{12,8},{9,13},{13,9},{1,5},{5,1},{2,6},{6,2},{1... | collective-permute-start | bytes 393224 | tf_op jit(solution)/shard_map/ppermute | solution.py:42
  139.1 1.0 collective-permute-done.12.refs_1_
  140.1 3.7 %collective-permute-done.13.refs_2_ = f32[32,8,128]{2,1,0:T(8,128)S(1)} collective-permute-done((f32[32,8,128]{2,1,0:T(8,128)S(1)}, f32[32,8,128]{2,1,0:T(8,128)S(1)}, u32[]{:S(2)}, u32[]{:S(2)}) %collective-permute-start.13) | collective-permute-done | bytes 131104 | tf_op jit(solution)/shard_map/ppermute | solution.py:42
  143.8 7.4 %shard_map.49 = f32[32,8,128]{2,1,0:T(8,128)S(1)} custom-call(f32[5]{0:T(128)S(1)} %convert_element_type.3.flags, f32[4,32,8,128]{3,2,1,0:T(8,128)S(1)} %all_to_all.30.r_c, f32[3,32,8,128]{3,2,1,0:T(8,128)S(1)} %collective-permute-done.9.r_i, f32[3,32,8,128]{3,2,1,0:T(8,128)S(1)} %collective-permute-done.10.r_o, f32[32,24,128]{2,1,0:T(8,128)S(1)} %get-tuple-element.18.hinv, ...), custom_call_target="tpu_custom_call" | custom-call | tf_op jit(solution)/shard_map/pallas_call | solution.py:310
  151.3 6.5 %collective-permute-done.14.refs_0_ = f32[32,8,128]{2,1,0:T(8,128)S(1)} collective-permute-done((f32[32,8,128]{2,1,0:T(8,128)S(1)}, f32[32,8,128]{2,1,0:T(8,128)S(1)}, u32[]{:S(2)}, u32[]{:S(2)}) %collective-permute-start.14) | collective-permute-done | bytes 131104 | tf_op jit(solution)/shard_map/ppermute | solution.py:380
  157.8 4.2 %collective-permute-start.15 = (f32[32,8,128]{2,1,0:T(8,128)S(1)}, f32[32,8,128]{2,1,0:T(8,128)S(1)}, u32[]{:S(2)}, u32[]{:S(2)}) collective-permute-start(f32[32,8,128]{2,1,0:T(8,128)S(1)} %collective-permute-done.14.refs_0_), channel_id=1, source_target_pairs={{0,4},{4,0},{8,12},{12,8},{9,13},{13,9},{1,5},{5,1},{2,6},{6,2},{1... | collective-permute-start | bytes 393224 | tf_op jit(solution)/shard_map/ppermute | solution.py:42
  162.1 1.0 collective-permute-done.15.refs_1_
  163.1 3.7 %collective-permute-done.16.refs_2_ = f32[32,8,128]{2,1,0:T(8,128)S(1)} collective-permute-done((f32[32,8,128]{2,1,0:T(8,128)S(1)}, f32[32,8,128]{2,1,0:T(8,128)S(1)}, u32[]{:S(2)}, u32[]{:S(2)}) %collective-permute-start.16) | collective-permute-done | bytes 131104 | tf_op jit(solution)/shard_map/ppermute | solution.py:42
  166.8 7.4 %shard_map.50 = f32[32,8,128]{2,1,0:T(8,128)S(1)} custom-call(f32[5]{0:T(128)S(1)} %convert_element_type.3.flags, f32[4,32,8,128]{3,2,1,0:T(8,128)S(1)} %all_to_all.30.r_c, f32[3,32,8,128]{3,2,1,0:T(8,128)S(1)} %collective-permute-done.9.r_i, f32[3,32,8,128]{3,2,1,0:T(8,128)S(1)} %collective-permute-done.10.r_o, f32[32,24,128]{2,1,0:T(8,128)S(1)} %get-tuple-element.18.hinv, ...), custom_call_target="tpu_custom_call" | custom-call | tf_op jit(solution)/shard_map/pallas_call | solution.py:310
  174.2 6.3 %collective-permute-done.17.refs_0_ = f32[32,8,128]{2,1,0:T(8,128)S(1)} collective-permute-done((f32[32,8,128]{2,1,0:T(8,128)S(1)}, f32[32,8,128]{2,1,0:T(8,128)S(1)}, u32[]{:S(2)}, u32[]{:S(2)}) %collective-permute-start.17) | collective-permute-done | bytes 131104 | tf_op jit(solution)/shard_map/ppermute | solution.py:380
  180.5 4.5 %collective-permute-start.18 = (f32[32,8,128]{2,1,0:T(8,128)S(1)}, f32[32,8,128]{2,1,0:T(8,128)S(1)}, u32[]{:S(2)}, u32[]{:S(2)}) collective-permute-start(f32[32,8,128]{2,1,0:T(8,128)S(1)} %collective-permute-done.17.refs_0_), channel_id=1, source_target_pairs={{0,4},{4,0},{8,12},{12,8},{9,13},{13,9},{1,5},{5,1},{2,6},{6,2},{1... | collective-permute-start | bytes 393224 | tf_op jit(solution)/shard_map/ppermute | solution.py:42
  185.0 1.0 collective-permute-done.18.refs_1_
  186.0 3.7 %collective-permute-done.19.refs_2_ = f32[32,8,128]{2,1,0:T(8,128)S(1)} collective-permute-done((f32[32,8,128]{2,1,0:T(8,128)S(1)}, f32[32,8,128]{2,1,0:T(8,128)S(1)}, u32[]{:S(2)}, u32[]{:S(2)}) %collective-permute-start.19) | collective-permute-done | bytes 131104 | tf_op jit(solution)/shard_map/ppermute | solution.py:42
  189.7 7.9 %shard_map.51 = f32[4,16,8,128]{3,2,1,0:T(8,128)S(1)} custom-call(f32[5]{0:T(128)S(1)} %convert_element_type.3.flags, f32[4,32,8,128]{3,2,1,0:T(8,128)S(1)} %all_to_all.30.r_c, f32[3,32,8,128]{3,2,1,0:T(8,128)S(1)} %collective-permute-done.9.r_i, f32[3,32,8,128]{3,2,1,0:T(8,128)S(1)} %collective-permute-done.10.r_o, ...), custom_call_target="tpu_custom_call" | custom-call | tf_op jit(solution)/shard_map/pallas_call | solution.py:310
  197.6 8.0 %all_to_all.31.d_c = f32[4,16,8,128]{3,2,1,0:T(8,128)S(1)} all-to-all(f32[4,16,8,128]{3,2,1,0:T(8,128)S(1)} %shard_map.51), channel_id=1, replica_groups={{0,16,32,48},{64,80,96,112},{128,144,160,176},{192,208,224,240},{1,17,3..., dimensions={0} | all-to-all | bytes 524288 | tf_op jit(solution)/shard_map/all_to_all | solution.py:388
  205.5 2.1 collective-permute-start.20
  207.6 1.2 collective-permute-done.20.d_i
  208.8 4.9 %collective-permute-done.21.d_o = f32[4,16,8,128]{3,2,1,0:T(8,128)S(1)} collective-permute-done((f32[4,16,8,128]{3,2,1,0:T(8,128)S(1)}, f32[4,16,8,128]{3,2,1,0:T(8,128)S(1)}, u32[]{:S(2)}, u32[]{:S(2)}) %collective-permute-start.21) | collective-permute-done | bytes 262176 | tf_op jit(solution)/shard_map/ppermute | solution.py:42
  213.7 13.0 %shard_map.52 = (f32[4,3,8,8,256]{4,3,2,1,0:T(8,128)S(1)}, f32[32,8,256]{2,1,0:T(8,128)S(1)}) custom-call(f32[5]{0:T(128)S(1)} %convert_element_type.3.flags, f32[4,16,8,128]{3,2,1,0:T(8,128)S(1)} %all_to_all.31.d_c, f32[4,16,8,128]{3,2,1,0:T(8,128)S(1)} %collective-permute-done.20.d_i, f32[4,16,8,128]{3,2,1,0:T(8,128)S(1)} %collective-permute-done.21.d_o, ...), custom_call_target="tpu_custom_call" | custom-call | tf_op jit(solution)/shard_map/pallas_call | solution.py:310
  226.7 1.0 collective-permute-start.22
  227.8 1.1 collective-permute-done.22.y_i
  228.9 4.9 %collective-permute-done.23.y_o = f32[32,8,256]{2,1,0:T(8,128)S(1)} collective-permute-done((f32[32,8,256]{2,1,0:T(8,128)S(1)}, f32[32,8,256]{2,1,0:T(8,128)S(1)}, u32[]{:S(2)}, u32[]{:S(2)}) %collective-permute-start.23) | collective-permute-done | bytes 262176 | tf_op jit(solution)/shard_map/ppermute | solution.py:42
  233.8 5.0 %shard_map.53 = f32[4,8,8,256]{3,2,1,0:T(8,128)S(1)} custom-call(f32[5]{0:T(128)S(1)} %convert_element_type.3.flags, f32[32,8,256]{2,1,0:T(8,128)S(1)} %get-tuple-element.23.y_c, f32[32,8,256]{2,1,0:T(8,128)S(1)} %collective-permute-done.22.y_i, f32[32,8,256]{2,1,0:T(8,128)S(1)} %collective-permute-done.23.y_o, f32[32,24,256]{2,1,0:T(8,128)S(1)} %get-tuple-element.16.fine, ...), custom_call_target="tpu_custom_call" | custom-call | tf_op jit(solution)/shard_map/pallas_call | solution.py:310
  238.9 16.9 %all_to_all.32 = f32[4,4,8,8,256]{4,3,2,1,0:T(8,128)S(1)} all-to-all(f32[4,4,8,8,256]{4,3,2,1,0:T(8,128)S(1)} %pad_maximum_fusion.1), channel_id=1, replica_groups=mesh['tm'=16,'sx'=4,'sy'=4] {'sx'}, dimensions={0} | all-to-all | bytes 2097152 | tf_op jit(solution)/shard_map/all_to_all | solution.py:403
  255.9 1.1 copy_bitcast_fusion
  (48 shorter events, 8.1 us)
Async XLA Ops:
  0.0 17.1 %collective-permute-start = (f32[8,32,256]{2,1,0:T(8,128)}, f32[8,32,256]{2,1,0:T(8,128)S(1)}, u32[]{:S(2)}, u32[]{:S(2)}) collective-permute-start(f32[8,32,256]{2,1,0:T(8,128)} %bitcast.45), channel_id=1, source_target_pairs={{0,16},{16,32},{32,48},{48,64},{64,80},{80,96},{96,112},{112,128},... | collective-permute-start | bytes 786440 | tf_op jit(solution)/shard_map/ppermute | solution.py:345
  18.1 1.0 copy-start.1
  19.0 8.4 %copy-start = (f32[4,8,32,256]{3,2,1,0:T(8,128)S(1)}, f32[4,8,32,256]{3,2,1,0:T(8,128)}, u32[]{:S(2)}) copy-start(f32[4,8,32,256]{3,2,1,0:T(8,128)} %param.6) | copy-start | bytes 3145732
  19.8 12.6 %all-to-all-start = ((f32[4,1,8,8,256]{4,3,2,1,0:T(8,128)}), f32[4,1,8,8,256]{4,3,2,1,0:T(8,128)S(1)}, u32[]{:S(2)}, u32[]{:S(2)}) async-start(f32[4,1,8,8,256]{4,3,2,1,0:T(8,128)} %copy.36), calls=%async_computation | async-start | bytes 524288 | tf_op jit(solution)/shard_map/all_to_all | solution.py:342
  27.4 1.0 copy-start.2
  29.5 7.4 %copy-start.3 = (f32[1,8,32,256]{3,2,1,0:T(8,128)S(1)}, f32[1,8,32,256]{3,2,1,0:T(8,128)}, u32[]{:S(2)}) copy-start(f32[1,8,32,256]{3,2,1,0:T(8,128)} %param.5) | copy-start | bytes 786436
  32.5 15.2 %all-to-all-start.1 = ((f32[4,3,8,8,256]{4,3,2,1,0:T(8,128)}), f32[4,3,8,8,256]{4,3,2,1,0:T(8,128)S(1)}, u32[]{:S(2)}, u32[]{:S(2)}) async-start(f32[4,3,8,8,256]{4,3,2,1,0:T(8,128)} %copy.37), calls=%async_computation.1 | async-start | bytes 1572864 | tf_op jit(solution)/shard_map/all_to_all | solution.py:342
  47.7 15.9 %all-to-all-start.2 = ((f32[4,3,8,8,256]{4,3,2,1,0:T(8,128)}), f32[4,3,8,8,256]{4,3,2,1,0:T(8,128)}, u32[]{:S(2)}, u32[]{:S(2)}) async-start(f32[4,3,8,8,256]{4,3,2,1,0:T(8,128)} %copy.38), calls=%async_computation.2 | async-start | bytes 1572864 | tf_op jit(solution)/shard_map/all_to_all | solution.py:342
  52.7 22.6 %collective-permute-start.3 = (f32[4,3,8,8,256]{4,3,2,1,0:T(8,128)S(1)}, f32[4,3,8,8,256]{4,3,2,1,0:T(8,128)S(1)}, u32[]{:S(2)}, u32[]{:S(2)}) collective-permute-start(f32[4,3,8,8,256]{4,3,2,1,0:T(8,128)S(1)} %all-to-all-done.1.s_c), channel_id=1, source_target_pairs={{0,4},{4,0},{8,12},{12,8},{9,13},{13,9},{1,5},{5,1},{2,6},{6,2},{1... | collective-permute-start | bytes 2359304 | tf_op jit(solution)/shard_map/ppermute | solution.py:42
  52.8 22.5 %collective-permute-start.4 = (f32[4,3,8,8,256]{4,3,2,1,0:T(8,128)S(1)}, f32[4,3,8,8,256]{4,3,2,1,0:T(8,128)S(1)}, u32[]{:S(2)}, u32[]{:S(2)}) collective-permute-start(f32[4,3,8,8,256]{4,3,2,1,0:T(8,128)S(1)} %all-to-all-done.1.s_c), channel_id=1, source_target_pairs={{0,7},{4,8},{8,4},{12,9},{9,12},{13,1},{1,13},{5,2},{2,5},{6,10},{... | collective-permute-start | bytes 2359304 | tf_op jit(solution)/shard_map/ppermute | solution.py:42
  54.5 11.2 %collective-permute-start.1 = (f32[32,8,256]{2,1,0:T(8,128)S(1)}, f32[32,8,256]{2,1,0:T(8,128)S(1)}, u32[]{:S(2)}, u32[]{:S(2)}) collective-permute-start(f32[32,8,256]{2,1,0:T(8,128)S(1)} %bitcast.39), channel_id=1, source_target_pairs={{0,4},{4,0},{8,12},{12,8},{9,13},{13,9},{1,5},{5,1},{2,6},{6,2},{1... | collective-permute-start | bytes 786440 | tf_op jit(solution)/shard_map/ppermute | solution.py:42
  55.7 19.6 %collective-permute-start.2 = (f32[32,8,256]{2,1,0:T(8,128)S(1)}, f32[32,8,256]{2,1,0:T(8,128)}, u32[]{:S(2)}, u32[]{:S(2)}) collective-permute-start(f32[32,8,256]{2,1,0:T(8,128)S(1)} %bitcast.40), channel_id=1, source_target_pairs={{0,7},{4,8},{8,4},{12,9},{9,12},{13,1},{1,13},{5,2},{2,5},{6,10},{... | collective-permute-start | bytes 786440 | tf_op jit(solution)/shard_map/ppermute | solution.py:42
  64.7 23.1 %collective-permute-start.7 = (f32[4,2,8,8,256]{4,3,2,1,0:T(8,128)S(1)}, f32[4,2,8,8,256]{4,3,2,1,0:T(8,128)}, u32[]{:S(2)}, u32[]{:S(2)}) collective-permute-start(f32[4,2,8,8,256]{4,3,2,1,0:T(8,128)S(1)} %slice.78.s_c), channel_id=1, source_target_pairs={{0,4},{4,0},{8,12},{12,8},{9,13},{13,9},{1,5},{5,1},{2,6},{6,2},{1... | collective-permute-start | bytes 1572872 | tf_op jit(solution)/shard_map/ppermute | solution.py:42
  65.7 22.2 %collective-permute-start.8 = (f32[4,2,8,8,256]{4,3,2,1,0:T(8,128)S(1)}, f32[4,2,8,8,256]{4,3,2,1,0:T(8,128)}, u32[]{:S(2)}, u32[]{:S(2)}) collective-permute-start(f32[4,2,8,8,256]{4,3,2,1,0:T(8,128)S(1)} %slice.78.s_c), channel_id=1, source_target_pairs={{0,7},{4,8},{8,4},{12,9},{9,12},{13,1},{1,13},{5,2},{2,5},{6,10},{... | collective-permute-start | bytes 1572872 | tf_op jit(solution)/shard_map/ppermute | solution.py:42
  86.3 1.6 collective-permute-start.5
  86.4 6.2 %collective-permute-start.6 = (f32[32,8,256]{2,1,0:T(8,128)S(1)}, f32[32,8,256]{2,1,0:T(8,128)S(1)}, u32[]{:S(2)}, u32[]{:S(2)}) collective-permute-start(f32[32,8,256]{2,1,0:T(8,128)S(1)} %get-tuple-element.15.v_c.w2), channel_id=1, source_target_pairs={{0,7},{4,8},{8,4},{12,9},{9,12},{13,1},{1,13},{5,2},{2,5},{6,10},{... | collective-permute-start | bytes 786440 | tf_op jit(solution)/shard_map/ppermute | solution.py:42
  113.8 8.4 %collective-permute-start.10 = (f32[3,32,8,128]{3,2,1,0:T(8,128)S(1)}, f32[3,32,8,128]{3,2,1,0:T(8,128)S(1)}, u32[]{:S(2)}, u32[]{:S(2)}) collective-permute-start(f32[3,32,8,128]{3,2,1,0:T(8,128)S(1)} %slice.80), channel_id=1, source_target_pairs={{0,7},{4,8},{8,4},{12,9},{9,12},{13,1},{1,13},{5,2},{2,5},{6,10},{... | collective-permute-start | bytes 1179656 | tf_op jit(solution)/shard_map/ppermute | solution.py:42
  116.4 5.8 %collective-permute-start.9 = (f32[3,32,8,128]{3,2,1,0:T(8,128)S(1)}, f32[3,32,8,128]{3,2,1,0:T(8,128)S(1)}, u32[]{:S(2)}, u32[]{:S(2)}) collective-permute-start(f32[3,32,8,128]{3,2,1,0:T(8,128)S(1)} %slice.80), channel_id=1, source_target_pairs={{0,4},{4,0},{8,12},{12,8},{9,13},{13,9},{1,5},{5,1},{2,6},{6,2},{1... | collective-permute-start | bytes 1179656 | tf_op jit(solution)/shard_map/ppermute | solution.py:42
  127.9 6.5 %collective-permute-start.11 = (f32[32,8,128]{2,1,0:T(8,128)S(1)}, f32[32,8,128]{2,1,0:T(8,128)S(1)}, u32[]{:S(2)}, u32[]{:S(2)}) collective-permute-start(f32[32,8,128]{2,1,0:T(8,128)S(1)} %shard_map.48), channel_id=1, source_target_pairs={{0,64},{16,80},{32,96},{48,112},{64,128},{80,144},{96,160},{112,17... | collective-permute-start | bytes 393224 | tf_op jit(solution)/shard_map/ppermute | solution.py:380
  134.3 5.8 %collective-permute-start.12 = (f32[32,8,128]{2,1,0:T(8,128)S(1)}, f32[32,8,128]{2,1,0:T(8,128)S(1)}, u32[]{:S(2)}, u32[]{:S(2)}) collective-permute-start(f32[32,8,128]{2,1,0:T(8,128)S(1)} %collective-permute-done.11.refs_0_), channel_id=1, source_target_pairs={{0,4},{4,0},{8,12},{12,8},{9,13},{13,9},{1,5},{5,1},{2,6},{6,2},{1... | collective-permute-start | bytes 393224 | tf_op jit(solution)/shard_map/ppermute | solution.py:42
  139.1 4.7 %collective-permute-start.13 = (f32[32,8,128]{2,1,0:T(8,128)S(1)}, f32[32,8,128]{2,1,0:T(8,128)S(1)}, u32[]{:S(2)}, u32[]{:S(2)}) collective-permute-start(f32[32,8,128]{2,1,0:T(8,128)S(1)} %collective-permute-done.11.refs_0_), channel_id=1, source_target_pairs={{0,7},{4,8},{8,4},{12,9},{9,12},{13,1},{1,13},{5,2},{2,5},{6,10},{... | collective-permute-start | bytes 393224 | tf_op jit(solution)/shard_map/ppermute | solution.py:42
  151.2 6.6 %collective-permute-start.14 = (f32[32,8,128]{2,1,0:T(8,128)S(1)}, f32[32,8,128]{2,1,0:T(8,128)S(1)}, u32[]{:S(2)}, u32[]{:S(2)}) collective-permute-start(f32[32,8,128]{2,1,0:T(8,128)S(1)} %shard_map.49), channel_id=1, source_target_pairs={{0,64},{16,80},{32,96},{48,112},{64,128},{80,144},{96,160},{112,17... | collective-permute-start | bytes 393224 | tf_op jit(solution)/shard_map/ppermute | solution.py:380
  157.8 5.2 %collective-permute-start.15 = (f32[32,8,128]{2,1,0:T(8,128)S(1)}, f32[32,8,128]{2,1,0:T(8,128)S(1)}, u32[]{:S(2)}, u32[]{:S(2)}) collective-permute-start(f32[32,8,128]{2,1,0:T(8,128)S(1)} %collective-permute-done.14.refs_0_), channel_id=1, source_target_pairs={{0,4},{4,0},{8,12},{12,8},{9,13},{13,9},{1,5},{5,1},{2,6},{6,2},{1... | collective-permute-start | bytes 393224 | tf_op jit(solution)/shard_map/ppermute | solution.py:42
  162.1 4.7 %collective-permute-start.16 = (f32[32,8,128]{2,1,0:T(8,128)S(1)}, f32[32,8,128]{2,1,0:T(8,128)S(1)}, u32[]{:S(2)}, u32[]{:S(2)}) collective-permute-start(f32[32,8,128]{2,1,0:T(8,128)S(1)} %collective-permute-done.14.refs_0_), channel_id=1, source_target_pairs={{0,7},{4,8},{8,4},{12,9},{9,12},{13,1},{1,13},{5,2},{2,5},{6,10},{... | collective-permute-start | bytes 393224 | tf_op jit(solution)/shard_map/ppermute | solution.py:42
  174.1 6.4 %collective-permute-start.17 = (f32[32,8,128]{2,1,0:T(8,128)S(1)}, f32[32,8,128]{2,1,0:T(8,128)S(1)}, u32[]{:S(2)}, u32[]{:S(2)}) collective-permute-start(f32[32,8,128]{2,1,0:T(8,128)S(1)} %shard_map.50), channel_id=1, source_target_pairs={{0,64},{16,80},{32,96},{48,112},{64,128},{80,144},{96,160},{112,17... | collective-permute-start | bytes 393224 | tf_op jit(solution)/shard_map/ppermute | solution.py:380
  180.5 5.5 %collective-permute-start.18 = (f32[32,8,128]{2,1,0:T(8,128)S(1)}, f32[32,8,128]{2,1,0:T(8,128)S(1)}, u32[]{:S(2)}, u32[]{:S(2)}) collective-permute-start(f32[32,8,128]{2,1,0:T(8,128)S(1)} %collective-permute-done.17.refs_0_), channel_id=1, source_target_pairs={{0,4},{4,0},{8,12},{12,8},{9,13},{13,9},{1,5},{5,1},{2,6},{6,2},{1... | collective-permute-start | bytes 393224 | tf_op jit(solution)/shard_map/ppermute | solution.py:42
  185.0 4.7 %collective-permute-start.19 = (f32[32,8,128]{2,1,0:T(8,128)S(1)}, f32[32,8,128]{2,1,0:T(8,128)S(1)}, u32[]{:S(2)}, u32[]{:S(2)}) collective-permute-start(f32[32,8,128]{2,1,0:T(8,128)S(1)} %collective-permute-done.17.refs_0_), channel_id=1, source_target_pairs={{0,7},{4,8},{8,4},{12,9},{9,12},{13,1},{1,13},{5,2},{2,5},{6,10},{... | collective-permute-start | bytes 393224 | tf_op jit(solution)/shard_map/ppermute | solution.py:42
  205.5 3.2 %collective-permute-start.20 = (f32[4,16,8,128]{3,2,1,0:T(8,128)S(1)}, f32[4,16,8,128]{3,2,1,0:T(8,128)S(1)}, u32[]{:S(2)}, u32[]{:S(2)}) collective-permute-start(f32[4,16,8,128]{3,2,1,0:T(8,128)S(1)} %all_to_all.31.d_c), channel_id=1, source_target_pairs={{0,4},{4,0},{8,12},{12,8},{9,13},{13,9},{1,5},{5,1},{2,6},{6,2},{1... | collective-permute-start | bytes 786440 | tf_op jit(solution)/shard_map/ppermute | solution.py:42
  207.6 6.1 %collective-permute-start.21 = (f32[4,16,8,128]{3,2,1,0:T(8,128)S(1)}, f32[4,16,8,128]{3,2,1,0:T(8,128)S(1)}, u32[]{:S(2)}, u32[]{:S(2)}) collective-permute-start(f32[4,16,8,128]{3,2,1,0:T(8,128)S(1)} %all_to_all.31.d_c), channel_id=1, source_target_pairs={{0,7},{4,8},{8,4},{12,9},{9,12},{13,1},{1,13},{5,2},{2,5},{6,10},{... | collective-permute-start | bytes 786440 | tf_op jit(solution)/shard_map/ppermute | solution.py:42
  226.7 2.2 collective-permute-start.22
  227.7 6.1 %collective-permute-start.23 = (f32[32,8,256]{2,1,0:T(8,128)S(1)}, f32[32,8,256]{2,1,0:T(8,128)S(1)}, u32[]{:S(2)}, u32[]{:S(2)}) collective-permute-start(f32[32,8,256]{2,1,0:T(8,128)S(1)} %get-tuple-element.23.y_c), channel_id=1, source_target_pairs={{0,7},{4,8},{8,4},{12,9},{9,12},{13,1},{1,13},{5,2},{2,5},{6,10},{... | collective-permute-start | bytes 786440 | tf_op jit(solution)/shard_map/ppermute | solution.py:42

commit v2 on v1

--- a/solution.py
+++ b/solution.py
@@ -42,7 +42,7 @@
     return lax.ppermute(value, axes, IN_CHIP), lax.ppermute(value, axes, OFF_CHIP)
 
 
-def sweep(source, target, hinv, rhs, closed):
+def sweep(source, target, hinv, saved, closed):
     width = source.shape[2]
     rows = source.shape[1]
     lane = lax.broadcasted_iota(jnp.int32, (rows, width), 1)
@@ -57,10 +57,10 @@
         low_y = pltpu.roll(here, 1, 0)
         high_y = pltpu.roll(here, rows - 1, 0)
         total = (source[x + 2] + WX * source[x]) + (high_y + WY * low_y) + (high_z + WZ * low_z)
-        target[x + 1] = (total + rhs(x, here)) * hinv[x]
+        target[x + 1] = (total + saved[x]) * hinv[x]
         return carry
 
-    lax.fori_loop(0, NX, body, 0, unroll=4)
+    lax.fori_loop(0, NX, body, 0, unroll=True)
 
 
 def clear_ends(*states):
@@ -81,19 +81,16 @@
         body(x)
         return carry
 
-    lax.fori_loop(0, NX, step, 0, unroll=2)
-
-
-def relax(a, b, hinv, saved, sweeps, closed, scale, extra=None):
-    def first(x, here):
-        value = scale * here if extra is None else scale * (here + extra(x))
-        saved[x] = value
-        return value
-
-    sweep(a, b, hinv, first, closed)
-    for index in range(1, sweeps):
-        source, target = (b, a) if index % 2 else (a, b)
-        sweep(source, target, hinv, lambda x, here: saved[x], closed)
+    lax.fori_loop(0, NX, step, 0, unroll=8)
+
+
+def relax(a, b, hinv, saved, pairs, closed):
+    def pair(index, carry):
+        sweep(a, b, hinv, saved, closed)
+        sweep(b, a, hinv, saved, closed)
+        return carry
+
+    lax.fori_loop(0, pairs, pair, 0)
 
 
 def centre_of(value):
@@ -109,9 +106,15 @@
     real = jnp.logical_and(row >= 0, row < 16 * ROWS)
     clear_ends(a, b)
 
+    def source(index, x):
+        hi, lo = x // 8, x % 8
+        return joined(fl, s_c[hi, index, lo], s_i[hi, index, lo], s_o[hi, index, lo])
+
     def fill(x):
         hi, lo = x // 8, x % 8
-        a[x + 1] = joined(fl, x_c[x], x_i[x], x_o[x])
+        value = joined(fl, x_c[x], x_i[x], x_o[x])
+        a[x + 1] = value
+        saved[x] = 2.0 * (value + source(1, x))
         absorb = joined(fl, s_c[hi, 0, lo], s_i[hi, 0, lo], s_o[hi, 0, lo])
         fine[x] = jnp.where(real, 0.5 / (5.0 + absorb), 0.0)
         value = jnp.where(real, 2.0 / (17.0 + 4.0 * absorb), 0.0)
@@ -119,46 +122,45 @@
         window[x] = jnp.where(inside, pltpu.roll(value, shift, 1)[:, :WINDOW], 0.0)
 
     each_x(fill)
-
-    def source(index):
-        def get(x):
-            hi, lo = x // 8, x % 8
-            return joined(fl, s_c[hi, index, lo], s_i[hi, index, lo], s_o[hi, index, lo])
-
-        return get
-
-    for index, out in ((1, w1), (2, w2)):
-        relax(a, b, fine, saved, 4, True, 2.0, source(index))
-
-        def put(x):
-            out[x] = centre_of(a[x + 1])
-
-        each_x(put)
+    relax(a, b, fine, saved, 2, True)
+
+    def turn(x):
+        value = a[x + 1]
+        w1[x] = centre_of(value)
+        saved[x] = 2.0 * (value + source(2, x))
+
+    each_x(turn)
+    relax(a, b, fine, saved, 2, True)
+
+    def put(x):
+        w2[x] = centre_of(a[x + 1])
+
+    each_x(put)
 
 
 def resid_kernel(flags, v_c, v_i, v_o, s_c, s_i, s_o, own, fine, w3, resid, chunks, a, b, saved):
     fl = [flags[k] for k in range(4)]
     clear_ends(a, b)
 
+    def source(index, x):
+        hi, lo = x // 8, x % 8
+        return joined(fl, s_c[hi, index, lo], s_i[hi, index, lo], s_o[hi, index, lo])
+
     def fill(x):
-        a[x + 1] = joined(fl, v_c[x], v_i[x], v_o[x])
+        value = joined(fl, v_c[x], v_i[x], v_o[x])
+        a[x + 1] = value
+        saved[x] = 2.0 * (value + source(0, x))
 
     each_x(fill)
-
-    def source(index):
-        def get(x):
-            hi, lo = x // 8, x % 8
-            return joined(fl, s_c[hi, index, lo], s_i[hi, index, lo], s_o[hi, index, lo])
-
-        return get
-
-    relax(a, b, fine, saved, 4, True, 2.0, source(0))
-
-    def put(x):
-        w3[x] = centre_of(a[x + 1])
-
-    each_x(put)
-    relax(a, b, fine, saved, 4, True, 2.0, source(1))
+    relax(a, b, fine, saved, 2, True)
+
+    def turn(x):
+        value = a[x + 1]
+        w3[x] = centre_of(value)
+        saved[x] = 2.0 * (value + source(1, x))
+
+    each_x(turn)
+    relax(a, b, fine, saved, 2, True)
     lane = lax.broadcasted_iota(jnp.int32, (ROWS, WINDOW), 1)
 
     def split(x):
@@ -192,11 +194,9 @@
         return jnp.concatenate([blank, r_c[step, x], blank], axis=0)
 
     def fill(x):
-        if first:
-            a[x + 1] = added(0, x)
-        else:
-            gate = flags[4]
-            a[x + 1] = gate * joined(fl, e_c[x], e_i[x], e_o[x])
+        value = added(0, x) if first else flags[4] * joined(fl, e_c[x], e_i[x], e_o[x])
+        a[x + 1] = value
+        saved[x] = 0.5 * value
 
     each_x(fill)
 
@@ -207,17 +207,19 @@
             out[step, x] = jnp.where(lane < PART, low, high)
             return carry
 
-        lax.fori_loop(0, NX // 2, put, 0, unroll=2)
+        lax.fori_loop(0, NX // 2, put, 0, unroll=8)
 
     for step in range(1 if first else 0, GROUP):
         if last:
             pack(step)
             if step == GROUP - 1:
                 return
-        relax(a, b, hinv, saved, 2, False, 0.5)
+        relax(a, b, hinv, saved, 1, False)
 
         def add(x):
-            a[x + 1] = a[x + 1] + added(step, x)
+            value = a[x + 1] + added(step, x)
+            a[x + 1] = value
+            saved[x] = 0.5 * value
 
         each_x(add)
 
@@ -256,25 +258,30 @@
             value = joined(fl, *values)
             a[x + half * index + 1] = value
             kept[x + half * index] = value
+            saved[x + half * index] = 0.5 * value
         return carry
 
-    lax.fori_loop(0, half, fill, 0)
-    relax(a, b, coarse, saved, 2, True, 0.5)
+    lax.fori_loop(0, half, fill, 0, unroll=4)
+    relax(a, b, coarse, saved, 1, True)
 
     def put(x):
         hi, lo = x // 8, x % 8
         out[hi, 2, lo] = (centre_of(a[x + 1]) + resid[x]) + own[hi, lo]
-        a[x + 1] = kept[x]
+        value = kept[x]
+        a[x + 1] = value
+        saved[x] = 2.0 * value
 
     each_x(put)
     for index, base in enumerate((w1, w2)):
-        relax(a, b, fine, saved, 4, True, 2.0)
+        relax(a, b, fine, saved, 2, True)
 
         def place(x):
             value = centre_of(a[x + 1])
             out[x // 8, index, x % 8] = value + base[x]
             if index == 1:
                 y2[x] = value
+            else:
+                saved[x] = 2.0 * a[x + 1]
 
         each_x(place)
 
@@ -284,10 +291,12 @@
     clear_ends(a, b)
 
     def fill(x):
-        a[x + 1] = joined(fl, y_c[x], y_i[x], y_o[x])
+        value = joined(fl, y_c[x], y_i[x], y_o[x])
+        a[x + 1] = value
+        saved[x] = 2.0 * value
 
     each_x(fill)
-    relax(a, b, fine, saved, 4, True, 2.0)
+    relax(a, b, fine, saved, 2, True)
 
     def put(x):
         out[x // 8, x % 8] = centre_of(a[x + 1]) + w3[x]

time: 258 us -> 223 us (0.86)
  Pallas kernels: 68.2 us -> 33.2 us
    pallas_call x8, Pallas kernels: 68.2 us -> 33.2 us  [call(): pl.pallas_call(kernel, out_shape=[jax.ShapeDtypeStruct(shape, F32) for sh...]
  transfers between devices with their start and end apart: 27 -> 27, of which waited for: 21 -> 21; matrix products, arithmetic and copies ran while one was open for 2% -> 2% of each run, Pallas kernels for 4% -> 3%
where the time goes in v2:
time: 223 us; the launch traced here: 222 us
  waiting for transfers between devices  97.3 us (44%)
  starting transfers between devices  46.5 us (21%)
  blocking collectives  35.1 us (16%)
  Pallas kernels  33.2 us (15%)
  local copies, waits for them, and re-layouts  6.93 us (3%)
  other arithmetic  2.64 us (1%)
    ppermute x10, waiting for transfers between devices, both_sides(): lax.ppermute(value, axes, OFF_CHIP)  37.8 us
    pallas_call x8, Pallas kernels, call(): pl.pallas_call(kernel, out_shape=[jax.ShapeDtypeStruct(shape, F32) for sh...  33.2 us
    ppermute x10, starting transfers between devices, both_sides(): lax.ppermute(value, axes, IN_CHIP)  21.8 us
    all_to_all x3, waiting for transfers between devices, to_blocks(): return lax.all_to_all(jnp.moveaxis(cut, 2, 0), 'sx', 0, 0)  20 us
    ppermute x3, waiting for transfers between devices, on_device(): lax.ppermute(state, 'tm', [(c, (c + GROUP) % 16) for c in range(16)])  19.2 us
    all_to_all x3, starting transfers between devices, to_blocks(): return lax.all_to_all(jnp.moveaxis(cut, 2, 0), 'sx', 0, 0)  17 us
    all_to_all x1, blocking collectives, on_device(): back = lax.all_to_all(fields, 'sx', 0, 0)  16.9 us
    ppermute x1, waiting for transfers between devices, on_device(): shifted = lax.ppermute(own, 'tm', [(c, (c + 1) % 16) for c in range(16)])  15 us
  transfers between devices with their start and end apart: 27, of which 21 were waited for; matrix products, arithmetic and copies ran while one was open for 2% of the time, Pallas kernels for 3%

profile of v2, /device:TPU:1, one launch (start us, length us, event | category | flops | bytes accessed | tf_op | source)
XLA Modules:
  0.0 222.0 jit_solution(13109419934675933262)
XLA Ops:
  0.0 2.1 collective-permute-start
  2.1 15.0 %collective-permute-done = f32[8,32,256]{2,1,0:T(8,128)S(1)} collective-permute-done((f32[8,32,256]{2,1,0:T(8,128)}, f32[8,32,256]{2,1,0:T(8,128)S(1)}, u32[]{:S(2)}, u32[]{:S(2)}) %collective-permute-start) | collective-permute-done | bytes 262176 | tf_op jit(solution)/shard_map/ppermute | solution.py:354
  17.1 1.0 select_bitcast_fusion
  19.8 7.6 %all-to-all-start = ((f32[4,1,8,8,256]{4,3,2,1,0:T(8,128)}), f32[4,1,8,8,256]{4,3,2,1,0:T(8,128)S(1)}, u32[]{:S(2)}, u32[]{:S(2)}) async-start(f32[4,1,8,8,256]{4,3,2,1,0:T(8,128)} %copy.36), calls=%async_computation | async-start | bytes 524288 | tf_op jit(solution)/shard_map/all_to_all | solution.py:351
  29.5 3.0 %all-to-all-done = f32[4,1,8,8,256]{4,3,2,1,0:T(8,128)S(1)} async-done(((f32[4,1,8,8,256]{4,3,2,1,0:T(8,128)}), f32[4,1,8,8,256]{4,3,2,1,0:T(8,128)S(1)}, u32[]{:S(2)}, u32[]{:S(2)}) %all-to-all-start) | async-done | bytes 262176 | tf_op jit(solution)/shard_map/all_to_all | solution.py:351
  32.5 4.4 %all-to-all-start.1 = ((f32[4,3,8,8,256]{4,3,2,1,0:T(8,128)}), f32[4,3,8,8,256]{4,3,2,1,0:T(8,128)S(1)}, u32[]{:S(2)}, u32[]{:S(2)}) async-start(f32[4,3,8,8,256]{4,3,2,1,0:T(8,128)} %copy.37), calls=%async_computation.1 | async-start | bytes 1572864 | tf_op jit(solution)/shard_map/all_to_all | solution.py:351
  37.1 1.0 copy.38
  38.1 9.6 %all-to-all-done.1.s_c = f32[4,3,8,8,256]{4,3,2,1,0:T(8,128)S(1)} async-done(((f32[4,3,8,8,256]{4,3,2,1,0:T(8,128)}), f32[4,3,8,8,256]{4,3,2,1,0:T(8,128)S(1)}, u32[]{:S(2)}, u32[]{:S(2)}) %all-to-all-start.1) | async-done | bytes 786464 | tf_op jit(solution)/shard_map/all_to_all | solution.py:351
  47.7 5.0 %all-to-all-start.2 = ((f32[4,3,8,8,256]{4,3,2,1,0:T(8,128)}), f32[4,3,8,8,256]{4,3,2,1,0:T(8,128)}, u32[]{:S(2)}, u32[]{:S(2)}) async-start(f32[4,3,8,8,256]{4,3,2,1,0:T(8,128)} %copy.38), calls=%async_computation.2 | async-start | bytes 1572864 | tf_op jit(solution)/shard_map/all_to_all | solution.py:351
  52.8 1.6 collective-permute-start.4
  54.5 1.2 collective-permute-start.1
  56.1 7.5 %all-to-all-done.2 = f32[4,3,8,8,256]{4,3,2,1,0:T(8,128)} async-done(((f32[4,3,8,8,256]{4,3,2,1,0:T(8,128)}), f32[4,3,8,8,256]{4,3,2,1,0:T(8,128)}, u32[]{:S(2)}, u32[]{:S(2)}) %all-to-all-start.2) | async-done | bytes 786464 | tf_op jit(solution)/shard_map/all_to_all | solution.py:351
  63.6 1.1 slice.78.s_c
  66.1 9.2 %collective-permute-done.2.x_o = f32[32,8,256]{2,1,0:T(8,128)} collective-permute-done((f32[32,8,256]{2,1,0:T(8,128)S(1)}, f32[32,8,256]{2,1,0:T(8,128)}, u32[]{:S(2)}, u32[]{:S(2)}) %collective-permute-start.2) | collective-permute-done | bytes 262176 | tf_op jit(solution)/shard_map/ppermute | solution.py:42
  75.3 6.1 %shard_map.46 = (f32[32,8,256]{2,1,0:T(8,128)S(1)}, f32[32,8,256]{2,1,0:T(8,128)S(1)}, f32[32,24,256]{2,1,0:T(8,128)S(1)}, f32[32,24,256]{2,1,0:T(8,128)S(1)}, f32[32,24,128]{2,1,0:T(8,128)S(1)}) custom-call(f32[5]{0:T(128)S(1)} %convert_element_type.3.flags, f32[32,8,256]{2,1,0:T(8,128)S(1)} %bitcast.41, f32[32,8,256]{2,1,0:T(8,128)S(1)} %collective-permute-done.1.x_i, ...), custom_call_target="tpu_custom_call" | custom-call | tf_op jit(solution)/shard_map/pallas_call | solution.py:319
  83.0 4.7 %collective-permute-done.6.v_o = f32[32,8,256]{2,1,0:T(8,128)S(1)} collective-permute-done((f32[32,8,256]{2,1,0:T(8,128)S(1)}, f32[32,8,256]{2,1,0:T(8,128)S(1)}, u32[]{:S(2)}, u32[]{:S(2)}) %collective-permute-start.6) | collective-permute-done | bytes 262176 | tf_op jit(solution)/shard_map/ppermute | solution.py:42
  87.7 6.3 %shard_map.47 = (f32[32,8,256]{2,1,0:T(8,128)S(1)}, f32[32,8,256]{2,1,0:T(8,128)S(1)}, f32[4,32,8,128]{3,2,1,0:T(8,128)S(1)}) custom-call(f32[5]{0:T(128)S(1)} %convert_element_type.3.flags, f32[32,8,256]{2,1,0:T(8,128)S(1)} %get-tuple-element.15.v_c.w2, f32[32,8,256]{2,1,0:T(8,128)S(1)} %collective-permute-done.5.v_i, ...), custom_call_target="tpu_custom_call" | custom-call | tf_op jit(solution)/shard_map/pallas_call | solution.py:319
  94.0 10.3 %all_to_all.30.r_c = f32[4,32,8,128]{3,2,1,0:T(8,128)S(1)} all-to-all(f32[4,32,8,128]{3,2,1,0:T(8,128)S(1)} %get-tuple-element.17), channel_id=1, replica_groups={{0,16,32,48},{64,80,96,112},{128,144,160,176},{192,208,224,240},{1,17,3..., dimensions={0} | all-to-all | bytes 1048576 | tf_op jit(solution)/shard_map/all_to_all | solution.py:381
  104.3 2.6 %collective-permute-start.10 = (f32[3,32,8,128]{3,2,1,0:T(8,128)S(1)}, f32[3,32,8,128]{3,2,1,0:T(8,128)S(1)}, u32[]{:S(2)}, u32[]{:S(2)}) collective-permute-start(f32[3,32,8,128]{3,2,1,0:T(8,128)S(1)} %slice.80), channel_id=1, source_target_pairs={{0,7},{4,8},{8,4},{12,9},{9,12},{13,1},{1,13},{5,2},{2,5},{6,10},{... | collective-permute-start | bytes 1179656 | tf_op jit(solution)/shard_map/ppermute | solution.py:42
  106.9 2.8 %collective-permute-start.9 = (f32[3,32,8,128]{3,2,1,0:T(8,128)S(1)}, f32[3,32,8,128]{3,2,1,0:T(8,128)S(1)}, u32[]{:S(2)}, u32[]{:S(2)}) collective-permute-start(f32[3,32,8,128]{3,2,1,0:T(8,128)S(1)} %slice.80), channel_id=1, source_target_pairs={{0,4},{4,0},{8,12},{12,8},{9,13},{13,9},{1,5},{5,1},{2,6},{6,2},{1... | collective-permute-start | bytes 1179656 | tf_op jit(solution)/shard_map/ppermute | solution.py:42
  109.7 3.0 %collective-permute-done.10.r_o = f32[3,32,8,128]{3,2,1,0:T(8,128)S(1)} collective-permute-done((f32[3,32,8,128]{3,2,1,0:T(8,128)S(1)}, f32[3,32,8,128]{3,2,1,0:T(8,128)S(1)}, u32[]{:S(2)}, u32[]{:S(2)}) %collective-permute-start.10) | collective-permute-done | bytes 393248 | tf_op jit(solution)/shard_map/ppermute | solution.py:42
  112.7 2.4 %shard_map.48 = f32[32,8,128]{2,1,0:T(8,128)S(1)} custom-call(f32[5]{0:T(128)S(1)} %convert_element_type.3.flags, f32[4,32,8,128]{3,2,1,0:T(8,128)S(1)} %all_to_all.30.r_c, f32[3,32,8,128]{3,2,1,0:T(8,128)S(1)} %collective-permute-done.9.r_i, f32[3,32,8,128]{3,2,1,0:T(8,128)S(1)} %collective-permute-done.10.r_o, f32[32,24,128]{2,1,0:T(8,128)S(1)} %get-tuple-element.18.hinv), custom_call_target="tpu_custom_call" | custom-call | tf_op jit(solution)/shard_map/pallas_call | solution.py:319
  115.1 6.4 %collective-permute-done.11.refs_0_ = f32[32,8,128]{2,1,0:T(8,128)S(1)} collective-permute-done((f32[32,8,128]{2,1,0:T(8,128)S(1)}, f32[32,8,128]{2,1,0:T(8,128)S(1)}, u32[]{:S(2)}, u32[]{:S(2)}) %collective-permute-start.11) | collective-permute-done | bytes 131104 | tf_op jit(solution)/shard_map/ppermute | solution.py:389
  121.5 4.8 %collective-permute-start.12 = (f32[32,8,128]{2,1,0:T(8,128)S(1)}, f32[32,8,128]{2,1,0:T(8,128)S(1)}, u32[]{:S(2)}, u32[]{:S(2)}) collective-permute-start(f32[32,8,128]{2,1,0:T(8,128)S(1)} %collective-permute-done.11.refs_0_), channel_id=1, source_target_pairs={{0,4},{4,0},{8,12},{12,8},{9,13},{13,9},{1,5},{5,1},{2,6},{6,2},{1... | collective-permute-start | bytes 393224 | tf_op jit(solution)/shard_map/ppermute | solution.py:42
  126.3 1.0 collective-permute-done.12.refs_1_
  127.3 3.7 %collective-permute-done.13.refs_2_ = f32[32,8,128]{2,1,0:T(8,128)S(1)} collective-permute-done((f32[32,8,128]{2,1,0:T(8,128)S(1)}, f32[32,8,128]{2,1,0:T(8,128)S(1)}, u32[]{:S(2)}, u32[]{:S(2)}) %collective-permute-start.13) | collective-permute-done | bytes 131104 | tf_op jit(solution)/shard_map/ppermute | solution.py:42
  131.0 2.9 %shard_map.49 = f32[32,8,128]{2,1,0:T(8,128)S(1)} custom-call(f32[5]{0:T(128)S(1)} %convert_element_type.3.flags, f32[4,32,8,128]{3,2,1,0:T(8,128)S(1)} %all_to_all.30.r_c, f32[3,32,8,128]{3,2,1,0:T(8,128)S(1)} %collective-permute-done.9.r_i, f32[3,32,8,128]{3,2,1,0:T(8,128)S(1)} %collective-permute-done.10.r_o, f32[32,24,128]{2,1,0:T(8,128)S(1)} %get-tuple-element.18.hinv, ...), custom_call_target="tpu_custom_call" | custom-call | tf_op jit(solution)/shard_map/pallas_call | solution.py:319
  134.0 6.5 %collective-permute-done.14.refs_0_ = f32[32,8,128]{2,1,0:T(8,128)S(1)} collective-permute-done((f32[32,8,128]{2,1,0:T(8,128)S(1)}, f32[32,8,128]{2,1,0:T(8,128)S(1)}, u32[]{:S(2)}, u32[]{:S(2)}) %collective-permute-start.14) | collective-permute-done | bytes 131104 | tf_op jit(solution)/shard_map/ppermute | solution.py:389
  140.5 4.2 %collective-permute-start.15 = (f32[32,8,128]{2,1,0:T(8,128)S(1)}, f32[32,8,128]{2,1,0:T(8,128)S(1)}, u32[]{:S(2)}, u32[]{:S(2)}) collective-permute-start(f32[32,8,128]{2,1,0:T(8,128)S(1)} %collective-permute-done.14.refs_0_), channel_id=1, source_target_pairs={{0,4},{4,0},{8,12},{12,8},{9,13},{13,9},{1,5},{5,1},{2,6},{6,2},{1... | collective-permute-start | bytes 393224 | tf_op jit(solution)/shard_map/ppermute | solution.py:42
  144.8 1.0 collective-permute-done.15.refs_1_
  145.8 3.7 %collective-permute-done.16.refs_2_ = f32[32,8,128]{2,1,0:T(8,128)S(1)} collective-permute-done((f32[32,8,128]{2,1,0:T(8,128)S(1)}, f32[32,8,128]{2,1,0:T(8,128)S(1)}, u32[]{:S(2)}, u32[]{:S(2)}) %collective-permute-start.16) | collective-permute-done | bytes 131104 | tf_op jit(solution)/shard_map/ppermute | solution.py:42
  149.5 2.9 %shard_map.50 = f32[32,8,128]{2,1,0:T(8,128)S(1)} custom-call(f32[5]{0:T(128)S(1)} %convert_element_type.3.flags, f32[4,32,8,128]{3,2,1,0:T(8,128)S(1)} %all_to_all.30.r_c, f32[3,32,8,128]{3,2,1,0:T(8,128)S(1)} %collective-permute-done.9.r_i, f32[3,32,8,128]{3,2,1,0:T(8,128)S(1)} %collective-permute-done.10.r_o, f32[32,24,128]{2,1,0:T(8,128)S(1)} %get-tuple-element.18.hinv, ...), custom_call_target="tpu_custom_call" | custom-call | tf_op jit(solution)/shard_map/pallas_call | solution.py:319
  152.5 6.3 %collective-permute-done.17.refs_0_ = f32[32,8,128]{2,1,0:T(8,128)S(1)} collective-permute-done((f32[32,8,128]{2,1,0:T(8,128)S(1)}, f32[32,8,128]{2,1,0:T(8,128)S(1)}, u32[]{:S(2)}, u32[]{:S(2)}) %collective-permute-start.17) | collective-permute-done | bytes 131104 | tf_op jit(solution)/shard_map/ppermute | solution.py:389
  158.8 4.5 %collective-permute-start.18 = (f32[32,8,128]{2,1,0:T(8,128)S(1)}, f32[32,8,128]{2,1,0:T(8,128)S(1)}, u32[]{:S(2)}, u32[]{:S(2)}) collective-permute-start(f32[32,8,128]{2,1,0:T(8,128)S(1)} %collective-permute-done.17.refs_0_), channel_id=1, source_target_pairs={{0,4},{4,0},{8,12},{12,8},{9,13},{13,9},{1,5},{5,1},{2,6},{6,2},{1... | collective-permute-start | bytes 393224 | tf_op jit(solution)/shard_map/ppermute | solution.py:42
  163.3 1.0 collective-permute-done.18.refs_1_
  164.3 3.7 %collective-permute-done.19.refs_2_ = f32[32,8,128]{2,1,0:T(8,128)S(1)} collective-permute-done((f32[32,8,128]{2,1,0:T(8,128)S(1)}, f32[32,8,128]{2,1,0:T(8,128)S(1)}, u32[]{:S(2)}, u32[]{:S(2)}) %collective-permute-start.19) | collective-permute-done | bytes 131104 | tf_op jit(solution)/shard_map/ppermute | solution.py:42
  168.0 2.8 %shard_map.51 = f32[4,16,8,128]{3,2,1,0:T(8,128)S(1)} custom-call(f32[5]{0:T(128)S(1)} %convert_element_type.3.flags, f32[4,32,8,128]{3,2,1,0:T(8,128)S(1)} %all_to_all.30.r_c, f32[3,32,8,128]{3,2,1,0:T(8,128)S(1)} %collective-permute-done.9.r_i, f32[3,32,8,128]{3,2,1,0:T(8,128)S(1)} %collective-permute-done.10.r_o, ...), custom_call_target="tpu_custom_call" | custom-call | tf_op jit(solution)/shard_map/pallas_call | solution.py:319
  170.8 7.9 %all_to_all.31.d_c = f32[4,16,8,128]{3,2,1,0:T(8,128)S(1)} all-to-all(f32[4,16,8,128]{3,2,1,0:T(8,128)S(1)} %shard_map.51), channel_id=1, replica_groups={{0,16,32,48},{64,80,96,112},{128,144,160,176},{192,208,224,240},{1,17,3..., dimensions={0} | all-to-all | bytes 524288 | tf_op jit(solution)/shard_map/all_to_all | solution.py:397
  178.8 2.1 collective-permute-start.20
  180.8 1.2 collective-permute-done.20.d_i
  182.0 4.9 %collective-permute-done.21.d_o = f32[4,16,8,128]{3,2,1,0:T(8,128)S(1)} collective-permute-done((f32[4,16,8,128]{3,2,1,0:T(8,128)S(1)}, f32[4,16,8,128]{3,2,1,0:T(8,128)S(1)}, u32[]{:S(2)}, u32[]{:S(2)}) %collective-permute-start.21) | collective-permute-done | bytes 262176 | tf_op jit(solution)/shard_map/ppermute | solution.py:42
  186.9 6.8 %shard_map.52 = (f32[4,3,8,8,256]{4,3,2,1,0:T(8,128)S(1)}, f32[32,8,256]{2,1,0:T(8,128)S(1)}) custom-call(f32[5]{0:T(128)S(1)} %convert_element_type.3.flags, f32[4,16,8,128]{3,2,1,0:T(8,128)S(1)} %all_to_all.31.d_c, f32[4,16,8,128]{3,2,1,0:T(8,128)S(1)} %collective-permute-done.20.d_i, f32[4,16,8,128]{3,2,1,0:T(8,128)S(1)} %collective-permute-done.21.d_o, ...), custom_call_target="tpu_custom_call" | custom-call | tf_op jit(solution)/shard_map/pallas_call | solution.py:319
  193.8 1.0 collective-permute-start.22
  194.9 1.1 collective-permute-done.22.y_i
  196.0 4.9 %collective-permute-done.23.y_o = f32[32,8,256]{2,1,0:T(8,128)S(1)} collective-permute-done((f32[32,8,256]{2,1,0:T(8,128)S(1)}, f32[32,8,256]{2,1,0:T(8,128)S(1)}, u32[]{:S(2)}, u32[]{:S(2)}) %collective-permute-start.23) | collective-permute-done | bytes 262176 | tf_op jit(solution)/shard_map/ppermute | solution.py:42
  200.9 2.9 %shard_map.53 = f32[4,8,8,256]{3,2,1,0:T(8,128)S(1)} custom-call(f32[5]{0:T(128)S(1)} %convert_element_type.3.flags, f32[32,8,256]{2,1,0:T(8,128)S(1)} %get-tuple-element.23.y_c, f32[32,8,256]{2,1,0:T(8,128)S(1)} %collective-permute-done.22.y_i, f32[32,8,256]{2,1,0:T(8,128)S(1)} %collective-permute-done.23.y_o, f32[32,24,256]{2,1,0:T(8,128)S(1)} %get-tuple-element.16.fine, ...), custom_call_target="tpu_custom_call" | custom-call | tf_op jit(solution)/shard_map/pallas_call | solution.py:319
  203.9 16.9 %all_to_all.32 = f32[4,4,8,8,256]{4,3,2,1,0:T(8,128)S(1)} all-to-all(f32[4,4,8,8,256]{4,3,2,1,0:T(8,128)S(1)} %pad_maximum_fusion.1), channel_id=1, replica_groups=mesh['tm'=16,'sx'=4,'sy'=4] {'sx'}, dimensions={0} | all-to-all | bytes 2097152 | tf_op jit(solution)/shard_map/all_to_all | solution.py:412
  220.9 1.1 copy_bitcast_fusion
  (48 shorter events, 8.1 us)
Async XLA Ops:
  0.0 17.1 %collective-permute-start = (f32[8,32,256]{2,1,0:T(8,128)}, f32[8,32,256]{2,1,0:T(8,128)S(1)}, u32[]{:S(2)}, u32[]{:S(2)}) collective-permute-start(f32[8,32,256]{2,1,0:T(8,128)} %bitcast.45), channel_id=1, source_target_pairs={{0,16},{16,32},{32,48},{48,64},{64,80},{80,96},{96,112},{112,128},... | collective-permute-start | bytes 786440 | tf_op jit(solution)/shard_map/ppermute | solution.py:354
  18.1 1.0 copy-start.1
  19.0 8.4 %copy-start = (f32[4,8,32,256]{3,2,1,0:T(8,128)S(1)}, f32[4,8,32,256]{3,2,1,0:T(8,128)}, u32[]{:S(2)}) copy-start(f32[4,8,32,256]{3,2,1,0:T(8,128)} %param.6) | copy-start | bytes 3145732
  19.8 12.6 %all-to-all-start = ((f32[4,1,8,8,256]{4,3,2,1,0:T(8,128)}), f32[4,1,8,8,256]{4,3,2,1,0:T(8,128)S(1)}, u32[]{:S(2)}, u32[]{:S(2)}) async-start(f32[4,1,8,8,256]{4,3,2,1,0:T(8,128)} %copy.36), calls=%async_computation | async-start | bytes 524288 | tf_op jit(solution)/shard_map/all_to_all | solution.py:351
  27.4 1.0 copy-start.2
  29.5 7.4 %copy-start.3 = (f32[1,8,32,256]{3,2,1,0:T(8,128)S(1)}, f32[1,8,32,256]{3,2,1,0:T(8,128)}, u32[]{:S(2)}) copy-start(f32[1,8,32,256]{3,2,1,0:T(8,128)} %param.5) | copy-start | bytes 786436
  32.5 15.2 %all-to-all-start.1 = ((f32[4,3,8,8,256]{4,3,2,1,0:T(8,128)}), f32[4,3,8,8,256]{4,3,2,1,0:T(8,128)S(1)}, u32[]{:S(2)}, u32[]{:S(2)}) async-start(f32[4,3,8,8,256]{4,3,2,1,0:T(8,128)} %copy.37), calls=%async_computation.1 | async-start | bytes 1572864 | tf_op jit(solution)/shard_map/all_to_all | solution.py:351
  47.7 15.9 %all-to-all-start.2 = ((f32[4,3,8,8,256]{4,3,2,1,0:T(8,128)}), f32[4,3,8,8,256]{4,3,2,1,0:T(8,128)}, u32[]{:S(2)}, u32[]{:S(2)}) async-start(f32[4,3,8,8,256]{4,3,2,1,0:T(8,128)} %copy.38), calls=%async_computation.2 | async-start | bytes 1572864 | tf_op jit(solution)/shard_map/all_to_all | solution.py:351
  52.7 22.6 %collective-permute-start.3 = (f32[4,3,8,8,256]{4,3,2,1,0:T(8,128)S(1)}, f32[4,3,8,8,256]{4,3,2,1,0:T(8,128)S(1)}, u32[]{:S(2)}, u32[]{:S(2)}) collective-permute-start(f32[4,3,8,8,256]{4,3,2,1,0:T(8,128)S(1)} %all-to-all-done.1.s_c), channel_id=1, source_target_pairs={{0,4},{4,0},{8,12},{12,8},{9,13},{13,9},{1,5},{5,1},{2,6},{6,2},{1... | collective-permute-start | bytes 2359304 | tf_op jit(solution)/shard_map/ppermute | solution.py:42
  52.8 22.5 %collective-permute-start.4 = (f32[4,3,8,8,256]{4,3,2,1,0:T(8,128)S(1)}, f32[4,3,8,8,256]{4,3,2,1,0:T(8,128)S(1)}, u32[]{:S(2)}, u32[]{:S(2)}) collective-permute-start(f32[4,3,8,8,256]{4,3,2,1,0:T(8,128)S(1)} %all-to-all-done.1.s_c), channel_id=1, source_target_pairs={{0,7},{4,8},{8,4},{12,9},{9,12},{13,1},{1,13},{5,2},{2,5},{6,10},{... | collective-permute-start | bytes 2359304 | tf_op jit(solution)/shard_map/ppermute | solution.py:42
  54.5 11.2 %collective-permute-start.1 = (f32[32,8,256]{2,1,0:T(8,128)S(1)}, f32[32,8,256]{2,1,0:T(8,128)S(1)}, u32[]{:S(2)}, u32[]{:S(2)}) collective-permute-start(f32[32,8,256]{2,1,0:T(8,128)S(1)} %bitcast.39), channel_id=1, source_target_pairs={{0,4},{4,0},{8,12},{12,8},{9,13},{13,9},{1,5},{5,1},{2,6},{6,2},{1... | collective-permute-start | bytes 786440 | tf_op jit(solution)/shard_map/ppermute | solution.py:42
  55.7 19.6 %collective-permute-start.2 = (f32[32,8,256]{2,1,0:T(8,128)S(1)}, f32[32,8,256]{2,1,0:T(8,128)}, u32[]{:S(2)}, u32[]{:S(2)}) collective-permute-start(f32[32,8,256]{2,1,0:T(8,128)S(1)} %bitcast.40), channel_id=1, source_target_pairs={{0,7},{4,8},{8,4},{12,9},{9,12},{13,1},{1,13},{5,2},{2,5},{6,10},{... | collective-permute-start | bytes 786440 | tf_op jit(solution)/shard_map/ppermute | solution.py:42
  64.7 18.2 %collective-permute-start.7 = (f32[4,2,8,8,256]{4,3,2,1,0:T(8,128)S(1)}, f32[4,2,8,8,256]{4,3,2,1,0:T(8,128)}, u32[]{:S(2)}, u32[]{:S(2)}) collective-permute-start(f32[4,2,8,8,256]{4,3,2,1,0:T(8,128)S(1)} %slice.78.s_c), channel_id=1, source_target_pairs={{0,4},{4,0},{8,12},{12,8},{9,13},{13,9},{1,5},{5,1},{2,6},{6,2},{1... | collective-permute-start | bytes 1572872 | tf_op jit(solution)/shard_map/ppermute | solution.py:42
  65.7 17.3 %collective-permute-start.8 = (f32[4,2,8,8,256]{4,3,2,1,0:T(8,128)S(1)}, f32[4,2,8,8,256]{4,3,2,1,0:T(8,128)}, u32[]{:S(2)}, u32[]{:S(2)}) collective-permute-start(f32[4,2,8,8,256]{4,3,2,1,0:T(8,128)S(1)} %slice.78.s_c), channel_id=1, source_target_pairs={{0,7},{4,8},{8,4},{12,9},{9,12},{13,1},{1,13},{5,2},{2,5},{6,10},{... | collective-permute-start | bytes 1572872 | tf_op jit(solution)/shard_map/ppermute | solution.py:42
  81.4 1.6 collective-permute-start.5
  81.5 6.2 %collective-permute-start.6 = (f32[32,8,256]{2,1,0:T(8,128)S(1)}, f32[32,8,256]{2,1,0:T(8,128)S(1)}, u32[]{:S(2)}, u32[]{:S(2)}) collective-permute-start(f32[32,8,256]{2,1,0:T(8,128)S(1)} %get-tuple-element.15.v_c.w2), channel_id=1, source_target_pairs={{0,7},{4,8},{8,4},{12,9},{9,12},{13,1},{1,13},{5,2},{2,5},{6,10},{... | collective-permute-start | bytes 786440 | tf_op jit(solution)/shard_map/ppermute | solution.py:42
  104.3 8.4 %collective-permute-start.10 = (f32[3,32,8,128]{3,2,1,0:T(8,128)S(1)}, f32[3,32,8,128]{3,2,1,0:T(8,128)S(1)}, u32[]{:S(2)}, u32[]{:S(2)}) collective-permute-start(f32[3,32,8,128]{3,2,1,0:T(8,128)S(1)} %slice.80), channel_id=1, source_target_pairs={{0,7},{4,8},{8,4},{12,9},{9,12},{13,1},{1,13},{5,2},{2,5},{6,10},{... | collective-permute-start | bytes 1179656 | tf_op jit(solution)/shard_map/ppermute | solution.py:42
  106.9 5.8 %collective-permute-start.9 = (f32[3,32,8,128]{3,2,1,0:T(8,128)S(1)}, f32[3,32,8,128]{3,2,1,0:T(8,128)S(1)}, u32[]{:S(2)}, u32[]{:S(2)}) collective-permute-start(f32[3,32,8,128]{3,2,1,0:T(8,128)S(1)} %slice.80), channel_id=1, source_target_pairs={{0,4},{4,0},{8,12},{12,8},{9,13},{13,9},{1,5},{5,1},{2,6},{6,2},{1... | collective-permute-start | bytes 1179656 | tf_op jit(solution)/shard_map/ppermute | solution.py:42
  115.0 6.5 %collective-permute-start.11 = (f32[32,8,128]{2,1,0:T(8,128)S(1)}, f32[32,8,128]{2,1,0:T(8,128)S(1)}, u32[]{:S(2)}, u32[]{:S(2)}) collective-permute-start(f32[32,8,128]{2,1,0:T(8,128)S(1)} %shard_map.48), channel_id=1, source_target_pairs={{0,64},{16,80},{32,96},{48,112},{64,128},{80,144},{96,160},{112,17... | collective-permute-start | bytes 393224 | tf_op jit(solution)/shard_map/ppermute | solution.py:389
  121.5 5.8 %collective-permute-start.12 = (f32[32,8,128]{2,1,0:T(8,128)S(1)}, f32[32,8,128]{2,1,0:T(8,128)S(1)}, u32[]{:S(2)}, u32[]{:S(2)}) collective-permute-start(f32[32,8,128]{2,1,0:T(8,128)S(1)} %collective-permute-done.11.refs_0_), channel_id=1, source_target_pairs={{0,4},{4,0},{8,12},{12,8},{9,13},{13,9},{1,5},{5,1},{2,6},{6,2},{1... | collective-permute-start | bytes 393224 | tf_op jit(solution)/shard_map/ppermute | solution.py:42
  126.3 4.7 %collective-permute-start.13 = (f32[32,8,128]{2,1,0:T(8,128)S(1)}, f32[32,8,128]{2,1,0:T(8,128)S(1)}, u32[]{:S(2)}, u32[]{:S(2)}) collective-permute-start(f32[32,8,128]{2,1,0:T(8,128)S(1)} %collective-permute-done.11.refs_0_), channel_id=1, source_target_pairs={{0,7},{4,8},{8,4},{12,9},{9,12},{13,1},{1,13},{5,2},{2,5},{6,10},{... | collective-permute-start | bytes 393224 | tf_op jit(solution)/shard_map/ppermute | solution.py:42
  133.9 6.6 %collective-permute-start.14 = (f32[32,8,128]{2,1,0:T(8,128)S(1)}, f32[32,8,128]{2,1,0:T(8,128)S(1)}, u32[]{:S(2)}, u32[]{:S(2)}) collective-permute-start(f32[32,8,128]{2,1,0:T(8,128)S(1)} %shard_map.49), channel_id=1, source_target_pairs={{0,64},{16,80},{32,96},{48,112},{64,128},{80,144},{96,160},{112,17... | collective-permute-start | bytes 393224 | tf_op jit(solution)/shard_map/ppermute | solution.py:389
  140.5 5.2 %collective-permute-start.15 = (f32[32,8,128]{2,1,0:T(8,128)S(1)}, f32[32,8,128]{2,1,0:T(8,128)S(1)}, u32[]{:S(2)}, u32[]{:S(2)}) collective-permute-start(f32[32,8,128]{2,1,0:T(8,128)S(1)} %collective-permute-done.14.refs_0_), channel_id=1, source_target_pairs={{0,4},{4,0},{8,12},{12,8},{9,13},{13,9},{1,5},{5,1},{2,6},{6,2},{1... | collective-permute-start | bytes 393224 | tf_op jit(solution)/shard_map/ppermute | solution.py:42
  144.8 4.7 %collective-permute-start.16 = (f32[32,8,128]{2,1,0:T(8,128)S(1)}, f32[32,8,128]{2,1,0:T(8,128)S(1)}, u32[]{:S(2)}, u32[]{:S(2)}) collective-permute-start(f32[32,8,128]{2,1,0:T(8,128)S(1)} %collective-permute-done.14.refs_0_), channel_id=1, source_target_pairs={{0,7},{4,8},{8,4},{12,9},{9,12},{13,1},{1,13},{5,2},{2,5},{6,10},{... | collective-permute-start | bytes 393224 | tf_op jit(solution)/shard_map/ppermute | solution.py:42
  152.4 6.4 %collective-permute-start.17 = (f32[32,8,128]{2,1,0:T(8,128)S(1)}, f32[32,8,128]{2,1,0:T(8,128)S(1)}, u32[]{:S(2)}, u32[]{:S(2)}) collective-permute-start(f32[32,8,128]{2,1,0:T(8,128)S(1)} %shard_map.50), channel_id=1, source_target_pairs={{0,64},{16,80},{32,96},{48,112},{64,128},{80,144},{96,160},{112,17... | collective-permute-start | bytes 393224 | tf_op jit(solution)/shard_map/ppermute | solution.py:389
  158.8 5.5 %collective-permute-start.18 = (f32[32,8,128]{2,1,0:T(8,128)S(1)}, f32[32,8,128]{2,1,0:T(8,128)S(1)}, u32[]{:S(2)}, u32[]{:S(2)}) collective-permute-start(f32[32,8,128]{2,1,0:T(8,128)S(1)} %collective-permute-done.17.refs_0_), channel_id=1, source_target_pairs={{0,4},{4,0},{8,12},{12,8},{9,13},{13,9},{1,5},{5,1},{2,6},{6,2},{1... | collective-permute-start | bytes 393224 | tf_op jit(solution)/shard_map/ppermute | solution.py:42
  163.3 4.7 %collective-permute-start.19 = (f32[32,8,128]{2,1,0:T(8,128)S(1)}, f32[32,8,128]{2,1,0:T(8,128)S(1)}, u32[]{:S(2)}, u32[]{:S(2)}) collective-permute-start(f32[32,8,128]{2,1,0:T(8,128)S(1)} %collective-permute-done.17.refs_0_), channel_id=1, source_target_pairs={{0,7},{4,8},{8,4},{12,9},{9,12},{13,1},{1,13},{5,2},{2,5},{6,10},{... | collective-permute-start | bytes 393224 | tf_op jit(solution)/shard_map/ppermute | solution.py:42
  178.8 3.2 %collective-permute-start.20 = (f32[4,16,8,128]{3,2,1,0:T(8,128)S(1)}, f32[4,16,8,128]{3,2,1,0:T(8,128)S(1)}, u32[]{:S(2)}, u32[]{:S(2)}) collective-permute-start(f32[4,16,8,128]{3,2,1,0:T(8,128)S(1)} %all_to_all.31.d_c), channel_id=1, source_target_pairs={{0,4},{4,0},{8,12},{12,8},{9,13},{13,9},{1,5},{5,1},{2,6},{6,2},{1... | collective-permute-start | bytes 786440 | tf_op jit(solution)/shard_map/ppermute | solution.py:42
  180.8 6.1 %collective-permute-start.21 = (f32[4,16,8,128]{3,2,1,0:T(8,128)S(1)}, f32[4,16,8,128]{3,2,1,0:T(8,128)S(1)}, u32[]{:S(2)}, u32[]{:S(2)}) collective-permute-start(f32[4,16,8,128]{3,2,1,0:T(8,128)S(1)} %all_to_all.31.d_c), channel_id=1, source_target_pairs={{0,7},{4,8},{8,4},{12,9},{9,12},{13,1},{1,13},{5,2},{2,5},{6,10},{... | collective-permute-start | bytes 786440 | tf_op jit(solution)/shard_map/ppermute | solution.py:42
  193.8 2.2 collective-permute-start.22
  194.8 6.1 %collective-permute-start.23 = (f32[32,8,256]{2,1,0:T(8,128)S(1)}, f32[32,8,256]{2,1,0:T(8,128)S(1)}, u32[]{:S(2)}, u32[]{:S(2)}) collective-permute-start(f32[32,8,256]{2,1,0:T(8,128)S(1)} %get-tuple-element.23.y_c), channel_id=1, source_target_pairs={{0,7},{4,8},{8,4},{12,9},{9,12},{13,1},{1,13},{5,2},{2,5},{6,10},{... | collective-permute-start | bytes 786440 | tf_op jit(solution)/shard_map/ppermute | solution.py:42
